TPU v7x, 128 devices: a whole 4x4x4 slice. The times are simulated.
128 devices in a mesh: ctx: 16 (over x, y), mp: 8 (over z, core).
Axes of the slice: x: 4, y: 4, z: 4, core: 2. Of those that a mesh axis runs over, the one named last changes fastest.
Arguments:
- tokens: bfloat16 [8192, 8192], P('ctx', 'mp'), may hold values from -12 to 12
- norm_gain: bfloat16 [8192], replicated, may hold values from 0.099609375 to 1.8984375
- router_weight: bfloat16 [8192], replicated, may hold values from -0.0625 to 0.0625
- query_weight: bfloat16 [8192, 4096], P('ctx', 'mp'), may hold values from -2 to 2
- key_weight: bfloat16 [8192, 1024], P('ctx', 'mp'), may hold values from -1 to 1
- value_weight: bfloat16 [8192, 1024], P('ctx', 'mp'), may hold values from -0.0625 to 0.0625
- out_weight: bfloat16 [4096, 8192], P('mp', 'ctx'), may hold values from -0.1875 to 0.1875
- mlp_gain: bfloat16 [8192], P('mp'), may hold values from 0.099609375 to 1.8984375
- gate_weight: bfloat16 [8192, 28672], P('mp', 'ctx'), may hold values from -0.0625 to 0.0625
- up_weight: bfloat16 [8192, 28672], P('mp', 'ctx'), may hold values from -0.0625 to 0.0625
- down_weight: bfloat16 [28672, 8192], P('ctx', 'mp'), may hold values from -0.0625 to 0.0625
- destination: int32 [8192], P('ctx'), may hold values from -1 to 1023, as said below
- kept_pos: int32 [1024], P('ctx'), may hold values from 0 to 8191, as said below
Outputs:
- layer_out: bfloat16 [8192, 8192], P('ctx', 'mp')
Inputs may be any that keep to these rules, and one draw needn't show every extreme that they name: A token that skips the block has -1. The kept tokens, counted in sequence order as k = 0, 1, ..., 1023, have destination (k mod 16) * 64 + (k div 16): owner k mod 16, slot k div 16 of that owner. Each shard of 512 tokens keeps from 32 to 96 tokens, and in every draw some shard keeps exactly 96; so at most 6 kept tokens of one shard have one owner, and that most is reached in every draw. kept_pos[destination[t]] = t for every kept token t.
All inputs are finite; a program needn't handle non-finite values.
Results may differ from a plain program's by a relative error of at most 0.0055.
Values may be sent and summed in bfloat16 or wider, within the bound.
A program may use at most 128 MiB of HBM per device.

v0:
```python
import jax
import jax.numpy as jnp
from jax import lax
from jax.sharding import PartitionSpec as P

HEAD_DIM = 128


def sent_to_all(shard, axis):
    count = lax.axis_size(axis)
    return lax.all_to_all(
        jnp.broadcast_to(shard[None], (count, *shard.shape)), axis, 0, 0, tiled=True
    )


def in_order(tiles, dim):
    tiles = jnp.moveaxis(tiles, 0, dim)
    dims = tiles.shape
    return tiles.reshape(*dims[:dim], dims[dim] * dims[dim + 1], *dims[dim + 2 :])


def collect(shard, axis, dim):
    tiles = sent_to_all(shard, axis)
    return in_order(tiles, dim)


def in_one_piece(arrays, axis, dim, along):
    both = jnp.concatenate(arrays, axis=along)
    result, at, done = (lax.all_gather(both, axis, axis=dim, tiled=True), 0, [])
    for a in arrays:
        done.append(lax.slice_in_dim(result, at, at + a.shape[along], axis=along))
        at += a.shape[along]
    return tuple(done)


def in_blocks(shard, dim, count):
    dims = shard.shape
    tiles = shard.reshape(*dims[:dim], count, dims[dim] // count, *dims[dim + 1 :])
    return jnp.moveaxis(tiles, dim, 0)


def sent_and_summed(shard, axis, dim):
    tiles = in_blocks(shard, dim, lax.axis_size(axis))
    arrived = lax.all_to_all(tiles, axis, split_axis=0, concat_axis=0, tiled=True)
    return arrived.astype(jnp.float32).sum(axis=0)


def taken_together(shard, axis):
    everything = sent_to_all(shard, axis)
    return jnp.sum(everything, axis=0)


def rotate(values, positions):
    half_dim = values.shape[-1] // 2
    exponent = jnp.arange(half_dim, dtype=jnp.float32) * (2.0 / values.shape[-1])
    frequency = 500000.0 ** (-exponent)
    angles = positions.astype(jnp.float32)[:, None] * frequency[None, :]
    cosine = jnp.cos(angles)[:, None, :]
    sine_part = jnp.sin(angles)[:, None, :]
    first_half = values[..., :half_dim]
    second_half = values[..., half_dim:]
    return jnp.concatenate(
        [
            first_half * cosine - second_half * sine_part,
            second_half * cosine + first_half * sine_part,
        ],
        axis=-1,
    )


def body(
    tokens,
    norm_gain,
    router_weight,
    query_weight,
    key_weight,
    value_weight,
    out_weight,
    mlp_gain,
    gate_weight,
    up_weight,
    down_weight,
    destination,
    kept_pos,
):
    ctx_count = lax.axis_size("ctx")
    mp_count = lax.axis_size("mp")
    my_index = lax.axis_index("ctx")
    tok_dev = tokens.shape[0]
    kept_dev = kept_pos.shape[0]
    feature_cols = tokens.shape[1]
    feature_total = feature_cols * mp_count
    capacity = (3 * kept_dev // 2 + ctx_count - 1) // ctx_count
    slots_all = ctx_count * capacity
    head_dim = HEAD_DIM
    query_cols = query_weight.shape[1]
    key_cols = key_weight.shape[1]
    kv_local = key_cols // head_dim
    q_local = query_cols // head_dim
    group_size = q_local // kv_local
    peer_ids = jnp.arange(ctx_count, dtype=jnp.int32)
    is_kept = destination >= 0
    owner_ids = destination // kept_dev
    slot_ids = destination % kept_dev
    kept_order = slot_ids * ctx_count + owner_ids
    first_order = jnp.min(jnp.where(is_kept, kept_order, ctx_count * kept_dev))
    first_slots = (first_order - peer_ids + ctx_count - 1) // ctx_count
    owner_match = owner_ids[:, None] == peer_ids[None, :]
    send_index = (
        owner_ids * capacity
        + slot_ids
        - jnp.sum(jnp.where(owner_match, first_slots[None, :], 0), axis=1)
    )
    send_index = jnp.where(is_kept, send_index, slots_all)
    token_ids = jnp.arange(tok_dev, dtype=jnp.int32)
    picked = jnp.full((slots_all,), tok_dev, jnp.int32).at[send_index].set(token_ids, mode="drop")
    outgoing = jnp.take(tokens, picked, axis=0, mode="fill", fill_value=0).reshape(
        ctx_count, capacity, feature_cols
    )
    incoming = lax.all_to_all(outgoing, "ctx", split_axis=0, concat_axis=0, tiled=True).reshape(
        slots_all, feature_cols
    )
    slot_range = jnp.arange(kept_dev, dtype=jnp.int32)
    source_ids = kept_pos // tok_dev
    source_match = source_ids[:, None] == peer_ids[None, :]
    first_from = jnp.min(jnp.where(source_match, slot_range[:, None], kept_dev), axis=0)
    recv_index = (
        source_ids * capacity
        + slot_range
        - jnp.sum(jnp.where(source_match, first_from[None, :], 0), axis=1)
    )
    local_rows = incoming[recv_index]
    full_rows = collect(local_rows, "mp", 1)
    raw_rows = full_rows.astype(jnp.float32)
    mean_square = jnp.mean(raw_rows * raw_rows, axis=-1, keepdims=True)
    normed = (raw_rows * lax.rsqrt(mean_square + 1e-05) * norm_gain.astype(jnp.float32)).astype(
        jnp.bfloat16
    )
    router_score = jax.nn.sigmoid(
        jnp.dot(full_rows, router_weight, preferred_element_type=jnp.float32)
    )
    pieces = in_one_piece((query_weight, key_weight, value_weight), "ctx", 0, 1)
    query_sum = jnp.dot(normed, pieces[0], preferred_element_type=jnp.float32)
    key_sum = jnp.dot(normed, pieces[1], preferred_element_type=jnp.float32)
    value_sum = jnp.dot(normed, pieces[2], preferred_element_type=jnp.float32)
    queries = rotate(query_sum.reshape(kept_dev, q_local, head_dim), kept_pos).astype(jnp.bfloat16)
    queries = queries.reshape(kept_dev, kv_local, group_size, head_dim)
    key_rows = (
        rotate(key_sum.reshape(kept_dev, kv_local, head_dim), kept_pos)
        .astype(jnp.bfloat16)
        .reshape(kept_dev, key_cols)
    )
    value_rows = value_sum.astype(jnp.bfloat16)
    query_order = slot_range * ctx_count + my_index
    softmax_scale = head_dim ** (-0.5)
    running_max = jnp.full((kept_dev, kv_local, group_size), -1e30, jnp.float32)
    key_piece, value_piece = in_one_piece((key_rows, value_rows), "ctx", 0, 1)
    piece_rows = key_piece.shape[0]
    key_piece = key_piece.reshape(piece_rows, kv_local, head_dim)
    value_piece = value_piece.reshape(piece_rows, kv_local, head_dim).astype(jnp.float32)
    row_ids = jnp.arange(piece_rows, dtype=jnp.int32)
    key_order = row_ids % kept_dev * ctx_count + row_ids // kept_dev
    allowed = (key_order[None, :] <= query_order[:, None])[:, None, None, :]
    scores = (
        jnp.einsum("qhgd,khd->qhgk", queries, key_piece, preferred_element_type=jnp.float32)
        * softmax_scale
    )
    scores = jnp.where(allowed, scores, -1e30)
    new_max = jnp.maximum(running_max, jnp.max(scores, axis=-1))
    weights = jnp.where(allowed, jnp.exp(scores - new_max[..., None]), 0.0)
    running_sum = jnp.sum(weights, axis=-1)
    weighted = jnp.einsum("qhgk,khd->qhgd", weights, value_piece)
    attended = (
        (weighted / running_sum[..., None]).reshape(kept_dev, query_cols).astype(jnp.bfloat16)
    )
    head_delta = jnp.dot(
        attended,
        lax.all_gather(out_weight, "ctx", axis=1, tiled=True),
        preferred_element_type=jnp.float32,
    )
    head_share = sent_and_summed(head_delta.astype(jnp.bfloat16), "mp", 1)
    mixed_share = local_rows.astype(jnp.float32) + head_share
    square_sum = taken_together(jnp.sum(mixed_share * mixed_share, axis=1), "mp")
    second_normed = (
        mixed_share
        * lax.rsqrt(square_sum / feature_total + 1e-05)[:, None]
        * mlp_gain.astype(jnp.float32)
    ).astype(jnp.bfloat16)
    every_normed = collect(second_normed, "ctx", 0)
    hidden_cols = gate_weight.shape[1]
    gate_block = jnp.dot(every_normed, gate_weight, preferred_element_type=jnp.float32)
    up_block = jnp.dot(every_normed, up_weight, preferred_element_type=jnp.float32)
    gate_up = lax.psum_scatter(
        jnp.concatenate([gate_block, up_block], axis=1).astype(jnp.bfloat16),
        "mp",
        scatter_dimension=0,
        tiled=True,
    ).astype(jnp.float32)
    hidden = (jax.nn.silu(gate_up[:, :hidden_cols]) * gate_up[:, hidden_cols:]).astype(jnp.bfloat16)
    mlp_partial = jnp.dot(
        lax.all_gather(hidden, "mp", axis=0, tiled=True),
        down_weight,
        preferred_element_type=jnp.float32,
    )
    mlp_share = sent_and_summed(mlp_partial.astype(jnp.bfloat16), "ctx", 0)
    update = (router_score[:, None] * (head_share + mlp_share)).astype(jnp.bfloat16)
    returning = (
        jnp.zeros((slots_all, feature_cols), jnp.bfloat16)
        .at[recv_index]
        .set(update)
        .reshape(ctx_count, capacity, feature_cols)
    )
    returned = lax.all_to_all(returning, "ctx", split_axis=0, concat_axis=0, tiled=True).reshape(
        slots_all, feature_cols
    )
    arriving = jnp.take(returned, send_index, axis=0, mode="fill", fill_value=0)
    return (tokens.astype(jnp.float32) + arriving.astype(jnp.float32)).astype(jnp.bfloat16)


def solution(mesh):
    in_specs = (
        P("ctx", "mp"),
        P(),
        P(),
        P("ctx", "mp"),
        P("ctx", "mp"),
        P("ctx", "mp"),
        P("mp", "ctx"),
        P("mp"),
        P("mp", "ctx"),
        P("mp", "ctx"),
        P("ctx", "mp"),
        P("ctx"),
        P("ctx"),
    )
    out_specs = P("ctx", "mp")
    return jax.shard_map(body, mesh=mesh, in_specs=in_specs, out_specs=out_specs, check_vma=False)
```

profile of v0, /device:TPU:32, one launch (start us, length us, event | category | flops | bytes accessed | tf_op | source)
XLA Modules:
  0.0 416.6 jit_solution(8131444847191503162)
XLA Ops:
  6.5 2.2 pad_maximum_fusion.1
  12.3 2.4 scatter_custom_fusion
  16.6 7.0 %all-to-all-start = ((bf16[16,6,1024]{2,1,0:T(8,128)(2,1)}), bf16[16,6,1024]{2,1,0:T(8,128)(2,1)S(1)}, u32[]{:S(2)}, u32[]{:S(2)}) async-start(bf16[16,6,1024]{2,1,0:T(8,128)(2,1)} %broadcast_select_fusion), calls=%async_computation | async-start | bytes 524288 | tf_op jit(solution)/shard_map/all_to_all | solution.py:120
  23.9 11.0 %all-to-all-done = bf16[16,6,1024]{2,1,0:T(8,128)(2,1)S(1)} async-done(((bf16[16,6,1024]{2,1,0:T(8,128)(2,1)}), bf16[16,6,1024]{2,1,0:T(8,128)(2,1)S(1)}, u32[]{:S(2)}, u32[]{:S(2)}) %all-to-all-start) | async-done | bytes 196640 | tf_op jit(solution)/shard_map/all_to_all | solution.py:120
  36.8 5.5 %all-to-all-start.1 = ((bf16[8,64,1024]{2,1,0:T(8,128)(2,1)}), bf16[8,64,1024]{2,1,0:T(8,128)(2,1)S(1)}, u32[]{:S(2)}, u32[]{:S(2)}) async-start(bf16[8,64,1024]{2,1,0:T(8,128)(2,1)} %broadcast_in_dim.161), calls=%async_computation.1 | async-start | bytes 2097152 | tf_op jit(solution)/shard_map/all_to_all | solution.py:11
  42.6 14.1 %all-to-all-done.1 = bf16[8,64,1024]{2,1,0:T(8,128)(2,1)S(1)} async-done(((bf16[8,64,1024]{2,1,0:T(8,128)(2,1)}), bf16[8,64,1024]{2,1,0:T(8,128)(2,1)S(1)}, u32[]{:S(2)}, u32[]{:S(2)}) %all-to-all-start.1) | async-done | bytes 1048608 | tf_op jit(solution)/shard_map/all_to_all | solution.py:11
  59.6 44.5 %all-gather.4.cloned.1.call-done = bf16[8192,768]{1,0:T(8,128)(2,1)} async-done(((bf16[512,768]{1,0:T(8,128)(2,1)}), bf16[8192,768]{1,0:T(8,128)(2,1)}) %all-gather.4.cloned.1.call-update) | async-done | bytes 12582928 | tf_op jit(solution)/shard_map/all_gather | solution.py:29
  104.2 7.3 %slice_bitcast_fusion = bf16[512,8192]{0,1:T(8,128)(2,1)} fusion(bf16[8192,768]{1,0:T(8,128)(2,1)} %all-gather.4.cloned.1.call-done), kind=kLoop, calls=%fused_computation.6 | loop fusion | bytes 16777216 | tf_op jit(solution)/shard_map/dot_general | solution.py:143
  111.4 12.1 %copy.32 = bf16[512,8192]{1,0:T(8,128)(2,1)} copy(bf16[512,8192]{0,1:T(8,128)(2,1)} %slice_bitcast_fusion) | data formatting | bytes 16777216 | tf_op jit(solution)/shard_map/dot_general | solution.py:143
  123.6 2.3 fusion.12
  126.1 2.7 fusion.15
  128.9 24.3 %all_gather.13 = bf16[1024,256]{1,0:T(8,128)(2,1)S(1)} all-gather(bf16[64,256]{1,0:T(8,128)(2,1)S(1)} %pad_maximum_fusion.2), channel_id=1, replica_groups=mesh['ctx'=16,'mp'=8] {'ctx'}, dimensions={0}, use_global_device_ids=true | all-gather | bytes 557056 | tf_op jit(solution)/shard_map/all_gather | solution.py:29
  153.2 2.7 fusion.62
  157.2 28.2 %all-gather.6.cloned.1.call-done = bf16[512,8192]{1,0:T(8,128)(2,1)} async-done(((bf16[512,512]{1,0:T(8,128)(2,1)}), bf16[512,8192]{1,0:T(8,128)(2,1)}) %all-gather.6.cloned.1.call-update) | async-done | bytes 8388624 | tf_op jit(solution)/shard_map/all_gather | solution.py:178
  185.4 4.9 %convolution_convert_fusion = bf16[64,8192]{1,0:T(8,128)(2,1)S(1)} fusion(bf16[512,8192]{1,0:T(8,128)(2,1)} %all-gather.6.cloned.1.call-done, bf16[8,8,4,128]{3,2,1,0:T(4,128)(2,1)S(1)} %bitcast.88), kind=kOutput, calls=%fused_computation.5 | convolution fusion | flops 537395200 | bytes 9502720 | tf_op jit(solution)/shard_map/dot_general | solution.py:176
  190.4 19.3 %all_to_all.36 = bf16[8,64,1024]{2,1,0:T(8,128)(2,1)S(1)} all-to-all(bf16[8,64,1024]{2,1,0:T(8,128)(2,1)S(1)} %bitcast.80), channel_id=1, replica_groups=mesh['ctx'=16,'mp'=8] {'mp'}, dimensions={0} | all-to-all | bytes 2097152 | tf_op jit(solution)/shard_map/all_to_all | solution.py:44
  210.7 4.7 %all-to-all-start.3 = ((f32[8,1,64]{2,1,0:T(1,128)}), f32[8,1,64]{2,1,0:T(1,128)S(1)}, u32[]{:S(2)}, u32[]{:S(2)}) async-start(f32[8,1,64]{2,1,0:T(1,128)} %broadcast_in_dim.166), calls=%async_computation.3 | async-start | bytes 8192 | tf_op jit(solution)/shard_map/all_to_all | solution.py:11
  215.4 3.8 all-to-all-done.3
  219.6 33.2 %all_to_all.37 = bf16[16,64,1024]{2,1,0:T(8,128)(2,1)S(1)} all-to-all(bf16[16,64,1024]{2,1,0:T(8,128)(2,1)S(1)} %broadcast_in_dim.167), channel_id=1, replica_groups=mesh['ctx'=16,'mp'=8] {'ctx'}, dimensions={0} | all-to-all | bytes 4194304 | tf_op jit(solution)/shard_map/all_to_all | solution.py:11
  252.8 4.1 convolution_convert_fusion.1
  257.0 5.4 %convolution_convert_fusion.2 = bf16[1024,1792]{1,0:T(8,128)(2,1)} fusion(bf16[1024,1024]{1,0:T(8,128)(2,1)S(1)} %bitcast.84, bf16[1024,1792]{1,0:T(8,128)(2,1)S(1)} %copy-done.7), kind=kOutput, calls=%fused_computation.10 | convolution fusion | flops 3759931392 | bytes 9437184 | tf_op jit(solution)/shard_map/dot_general | solution.py:191
  262.4 5.6 %pad_maximum_fusion = bf16[1024,3584]{1,0:T(8,128)(2,1)} fusion(bf16[1024,1792]{1,0:T(8,128)(2,1)S(1)} %convolution_convert_fusion.1, bf16[1024,1792]{1,0:T(8,128)(2,1)} %convolution_convert_fusion.2), kind=kLoop, calls=%fused_computation.7 | loop fusion | flops 14680064 | bytes 14680064 | tf_op jit(solution)/shard_map/concatenate | solution.py:194
  268.0 42.5 %reduce-scatter.2.cloned.1.call-done = bf16[128,3584]{1,0:T(8,128)(2,1)} async-done(((bf16[1024,3584]{1,0:T(8,128)(2,1)}), bf16[128,3584]{1,0:T(8,128)(2,1)}) %reduce-scatter.2.cloned.1.call-update) | async-done | bytes 917520 | tf_op jit(solution)/shard_map/reduce_scatter | solution.py:193
  313.0 31.1 %all-gather.8.cloned.1.call-done = bf16[1024,1792]{1,0:T(8,128)(2,1)} async-done(((bf16[128,1792]{1,0:T(8,128)(2,1)}), bf16[1024,1792]{1,0:T(8,128)(2,1)}) %all-gather.8.cloned.1.call-update) | async-done | bytes 3670032 | tf_op jit(solution)/shard_map/all_gather | solution.py:201
  344.1 8.4 %convolution_convert_fusion.3 = bf16[1024,1024]{1,0:T(8,128)(2,1)} fusion(bf16[1024,1792]{1,0:T(8,128)(2,1)} %all-gather.8.cloned.1.call-done, bf16[1792,1024]{1,0:T(8,128)(2,1)} %param.23), kind=kOutput, calls=%fused_computation.23 | convolution fusion | flops 3759144960 | bytes 9437184 | tf_op jit(solution)/shard_map/dot_general | solution.py:200
  352.5 6.9 %all-to-all-start.5 = ((bf16[16,64,1024]{2,1,0:T(8,128)(2,1)}), bf16[16,64,1024]{2,1,0:T(8,128)(2,1)S(1)}, u32[]{:S(2)}, u32[]{:S(2)}) async-start(bf16[16,64,1024]{2,1,0:T(8,128)(2,1)} %bitcast.82), calls=%async_computation.6 | async-start | bytes 4194304 | tf_op jit(solution)/shard_map/all_to_all | solution.py:44
  359.5 1.6 fusion.21
  361.1 29.3 %all-to-all-done.5 = bf16[16,64,1024]{2,1,0:T(8,128)(2,1)S(1)} async-done(((bf16[16,64,1024]{2,1,0:T(8,128)(2,1)}), bf16[16,64,1024]{2,1,0:T(8,128)(2,1)S(1)}, u32[]{:S(2)}, u32[]{:S(2)}) %all-to-all-start.5) | async-done | bytes 2097184 | tf_op jit(solution)/shard_map/all_to_all | solution.py:44
  391.5 1.4 scatter_custom_fusion.1
  393.7 4.4 %all-to-all-start.6 = ((bf16[16,6,1024]{2,1,0:T(8,128)(2,1)}), bf16[16,6,1024]{2,1,0:T(8,128)(2,1)S(1)}, u32[]{:S(2)}, u32[]{:S(2)}) async-start(bf16[16,6,1024]{2,1,0:T(8,128)(2,1)} %reshape.341), calls=%async_computation.7 | async-start | bytes 524288 | tf_op jit(solution)/shard_map/all_to_all | solution.py:213
  398.1 8.5 %all-to-all-done.6 = bf16[16,6,1024]{2,1,0:T(8,128)(2,1)S(1)} async-done(((bf16[16,6,1024]{2,1,0:T(8,128)(2,1)}), bf16[16,6,1024]{2,1,0:T(8,128)(2,1)S(1)}, u32[]{:S(2)}, u32[]{:S(2)}) %all-to-all-start.6) | async-done | bytes 196640 | tf_op jit(solution)/shard_map/all_to_all | solution.py:213
  406.7 2.1 gather_fusion.2
  (84 shorter events, 19.4 us)
Async XLA Ops:
  6.5 8.2 %copy-start.1 = (bf16[512,1024]{1,0:T(8,128)(2,1)S(1)}, bf16[512,1024]{1,0:T(8,128)(2,1)}, u32[]{:S(2)}) copy-start(bf16[512,1024]{1,0:T(8,128)(2,1)} %param.13) | copy-start | bytes 3145732
  6.5 17.1 %copy-start.8 = (s32[64]{0:T(128)S(1)}, s32[64]{0:T(128)}, u32[]{:S(2)}) copy-start(s32[64]{0:T(128)} %param.25) | copy-start | bytes 772
  6.5 97.6 %all-gather.4.cloned.1.call-start = ((), (), s32[]{:S(2)}) async-start(), calls=%async_computation.8 | async-start | bytes 13369344 | tf_op jit(solution)/shard_map/all_gather | solution.py:29
  8.8 176.6 %all-gather.6.cloned.1.call-start = ((), (), s32[]{:S(2)}) async-start(), calls=%async_computation.9 | async-start | bytes 8912896 | tf_op jit(solution)/shard_map/all_gather | solution.py:178
  14.8 27.5 %copy-start.3 = (bf16[8192]{0:T(1024)(128)(2,1)S(1)}, bf16[8192]{0:T(1024)(128)(2,1)}, u32[]{:S(2)}) copy-start(bf16[8192]{0:T(1024)(128)(2,1)} %param.14) | copy-start | bytes 49156
  16.6 18.3 %all-to-all-start = ((bf16[16,6,1024]{2,1,0:T(8,128)(2,1)}), bf16[16,6,1024]{2,1,0:T(8,128)(2,1)S(1)}, u32[]{:S(2)}, u32[]{:S(2)}) async-start(bf16[16,6,1024]{2,1,0:T(8,128)(2,1)} %broadcast_select_fusion), calls=%async_computation | async-start | bytes 524288 | tf_op jit(solution)/shard_map/all_to_all | solution.py:120
  36.8 20.0 %all-to-all-start.1 = ((bf16[8,64,1024]{2,1,0:T(8,128)(2,1)}), bf16[8,64,1024]{2,1,0:T(8,128)(2,1)S(1)}, u32[]{:S(2)}, u32[]{:S(2)}) async-start(bf16[8,64,1024]{2,1,0:T(8,128)(2,1)} %broadcast_in_dim.161), calls=%async_computation.1 | async-start | bytes 2097152 | tf_op jit(solution)/shard_map/all_to_all | solution.py:11
  111.4 12.1 %copy-start.2 = (bf16[8,8,8,1024]{3,2,0,1:T(8,128)(2,1)S(1)}, bf16[8,8,8,1024]{3,2,0,1:T(8,128)(2,1)}, u32[]{:S(2)}) copy-start(bf16[8,8,8,1024]{3,2,0,1:T(8,128)(2,1)} %copy.37) | copy-start | bytes 3145732
  123.6 29.6 %copy-start = (bf16[512,8192]{1,0:T(8,128)(2,1)S(1)}, bf16[512,8192]{1,0:T(8,128)(2,1)}, u32[]{:S(2)}) copy-start(bf16[512,8192]{1,0:T(8,128)(2,1)} %copy.32) | copy-start | bytes 25165828
  190.3 25.1 %copy-start.5 = (bf16[1024]{0:T(1024)(128)(2,1)S(1)}, bf16[1024]{0:T(1024)(128)(2,1)}, u32[]{:S(2)}) copy-start(bf16[1024]{0:T(1024)(128)(2,1)} %param.20) | copy-start | bytes 6148
  210.7 8.5 %all-to-all-start.3 = ((f32[8,1,64]{2,1,0:T(1,128)}), f32[8,1,64]{2,1,0:T(1,128)S(1)}, u32[]{:S(2)}, u32[]{:S(2)}) async-start(f32[8,1,64]{2,1,0:T(1,128)} %broadcast_in_dim.166), calls=%async_computation.3 | async-start | bytes 8192 | tf_op jit(solution)/shard_map/all_to_all | solution.py:11
  215.4 95.1 %reduce-scatter.2.cloned.1.call-start = ((), (), s32[]{:S(2)}) async-start(), calls=%async_computation.10 | async-start | bytes 8257536 | tf_op jit(solution)/shard_map/reduce_scatter | solution.py:193
  219.2 33.6 %copy-start.6 = (bf16[1024,1792]{1,0:T(8,128)(2,1)S(1)}, bf16[1024,1792]{1,0:T(8,128)(2,1)}, u32[]{:S(2)}) copy-start(bf16[1024,1792]{1,0:T(8,128)(2,1)} %param.22) | copy-start | bytes 11010052
  252.8 4.2 copy-start.7
  268.0 76.1 %all-gather.8.cloned.1.call-start = ((), (), s32[]{:S(2)}) async-start(), calls=%async_computation.11 | async-start | bytes 4128768 | tf_op jit(solution)/shard_map/all_gather | solution.py:201
  352.5 7.0 %copy-start.4 = (bf16[8192]{0:T(1024)(128)(2,1)S(1)}, bf16[8192]{0:T(1024)(128)(2,1)}, u32[]{:S(2)}) copy-start(bf16[8192]{0:T(1024)(128)(2,1)} %param.15) | copy-start | bytes 49156
  352.5 37.9 %all-to-all-start.5 = ((bf16[16,64,1024]{2,1,0:T(8,128)(2,1)}), bf16[16,64,1024]{2,1,0:T(8,128)(2,1)S(1)}, u32[]{:S(2)}, u32[]{:S(2)}) async-start(bf16[16,64,1024]{2,1,0:T(8,128)(2,1)} %bitcast.82), calls=%async_computation.6 | async-start | bytes 4194304 | tf_op jit(solution)/shard_map/all_to_all | solution.py:44
  393.7 12.9 %all-to-all-start.6 = ((bf16[16,6,1024]{2,1,0:T(8,128)(2,1)}), bf16[16,6,1024]{2,1,0:T(8,128)(2,1)S(1)}, u32[]{:S(2)}, u32[]{:S(2)}) async-start(bf16[16,6,1024]{2,1,0:T(8,128)(2,1)} %reshape.341), calls=%async_computation.7 | async-start | bytes 524288 | tf_op jit(solution)/shard_map/all_to_all | solution.py:213
Sparse Core Ops, SparseCore 0:
  9.5 94.5 all-gather.3
  106.3 79.0 all-gather.5
  268.1 42.4 reduce-scatter.1
  313.1 30.9 all-gather.7
where the time goes:
time: 419 us; the launch traced here: 417 us
  waiting for transfers between devices  214 us (51%)
  blocking collectives  76.8 us (18%)
  matrix products  33 us (8%)
  local copies, waits for them, and re-layouts  30.8 us (7%)
  starting transfers between devices  28.7 us (7%)
  other arithmetic  20 us (5%)
  between operations  13.5 us (3%)
    all_gather x1, waiting for transfers between devices, in_one_piece(): result, at, done = (lax.all_gather(both, axis, axis=dim, tiled=True), 0, [])  44.5 us
    reduce_scatter x1, waiting for transfers between devices, body(): lax.psum_scatter(jnp.concatenate([gate_block, up_block], axis=1).astype(j...  42.5 us
    all_to_all x1, blocking collectives, sent_to_all(): lax.all_to_all(jnp.broadcast_to(shard[None], (count, *shard.shape)), axis...  33.2 us
    all_gather x1, waiting for transfers between devices, body(): lax.all_gather(hidden, 'mp', axis=0, tiled=True)  31.1 us
    all_to_all x1, waiting for transfers between devices, sent_and_summed(): lax.all_to_all(tiles, axis, split_axis=0, concat_axis=0, tiled=True)  29.3 us
    all_gather x1, waiting for transfers between devices, body(): lax.all_gather(out_weight, 'ctx', axis=1, tiled=True)  28.2 us
    all_gather x1, blocking collectives, in_one_piece(): result, at, done = (lax.all_gather(both, axis, axis=dim, tiled=True), 0, [])  24.3 us
    dot_general x2, local copies, waits for them, and re-layouts, body(): query_sum = jnp.dot(normed, pieces[0], preferred_element_type=jnp.float32)  19.4 us
  transfers between devices with their start and end apart: 9, of which 9 were waited for; matrix products, arithmetic and copies ran while one was open for 10% of the time, Pallas kernels for 0%

commit v1 on v0

--- a/solution.py
+++ b/solution.py
@@ -1,9 +1,394 @@
+import functools
+
 import jax
 import jax.numpy as jnp
 from jax import lax
 from jax.sharding import PartitionSpec as P
 
+from jax.experimental import pallas as pl
+from jax.experimental.pallas import tpu as pltpu
+
 HEAD_DIM = 128
+MESH = pl.DeviceIdType.MESH
+EPS = 1e-05
+
+
+def remote(source, target, sent, landed, device):
+    return pltpu.make_async_remote_copy(
+        src_ref=source,
+        dst_ref=target,
+        send_sem=sent,
+        recv_sem=landed,
+        device_id=device,
+        device_id_type=MESH,
+    )
+
+
+def mlp_kernel(
+    x_ref,
+    inv_gain_ref,
+    gate_ref,
+    up_ref,
+    down_ref,
+    out_ref,
+    own_x,
+    sib_x,
+    sib_gain,
+    weight,
+    down,
+    part,
+    sums,
+    hidden,
+    delta,
+    deltas,
+    load_sem,
+    swap_send,
+    swap_recv,
+    x_send,
+    x_recv,
+    pass_send,
+    pass_recv,
+    sum_send,
+    sum_recv,
+    hid_send,
+    hid_recv,
+    hop_send,
+    hop_recv,
+    out_send,
+    out_recv,
+):
+    rows, feats = x_ref.shape
+    half = gate_ref.shape[1] // 2
+    both = 2 * half
+    group = 4 * rows
+    c, m = lax.axis_index("ctx"), lax.axis_index("mp")
+    x, y = c // 4, c % 4
+    z, core = m // 2, m % 2
+    sibling = (c, z * 2 + 1 - core)
+
+    def peer(step):
+        turn = step // 4
+        shift = turn + (turn // 2) * (1 - 2 * (turn % 2))
+        return lax.rem(x + 4 - shift, 4) * 4 + lax.rem(y + step % 4, 4)
+
+    def z_peer(step):
+        return lax.rem(z + step, 4)
+
+    def group_of(turn):
+        shift = turn + (turn // 2) * (1 - 2 * (turn % 2))
+        return lax.rem(x + shift, 4)
+
+    barrier = pltpu.get_barrier_semaphore()
+
+    @pl.loop(1, 16)
+    def _(k):
+        pl.semaphore_signal(barrier, inc=1, device_id=(peer(k), m), device_id_type=MESH)
+
+    for k in range(1, 4):
+        pl.semaphore_signal(
+            barrier, inc=1, device_id=(c, z_peer(k) * 2 + core), device_id_type=MESH
+        )
+    pl.semaphore_signal(barrier, inc=1, device_id=sibling, device_id_type=MESH)
+
+    mine = pl.multiple_of(core * half, 128)
+    others = pl.multiple_of((1 - core) * half, 128)
+    loads = [
+        pltpu.make_async_copy(
+            gate_ref.at[:, pl.ds(mine, half)],
+            weight.at[pl.ds(0, feats), pl.ds(0, half)],
+            load_sem.at[0],
+        ),
+        pltpu.make_async_copy(
+            up_ref.at[:, pl.ds(mine, half)],
+            weight.at[pl.ds(0, feats), pl.ds(half, half)],
+            load_sem.at[1],
+        ),
+        pltpu.make_async_copy(down_ref, down, load_sem.at[2]),
+    ]
+    for load in loads:
+        load.start()
+    my_rows = pl.ds(pl.multiple_of(c * rows, rows), rows)
+    own_x[my_rows, :] = x_ref[...]
+    pl.semaphore_wait(barrier, 19)
+
+    def x_copy(who, device):
+        place = pl.ds(pl.multiple_of(who * rows, rows), rows)
+        return remote(own_x.at[place], own_x.at[place], x_send.at[who], x_recv.at[who], device)
+
+    def x_out(k):
+        return remote(
+            own_x.at[my_rows], own_x.at[my_rows], x_send.at[k], x_recv.at[c], (peer(k), m)
+        )
+
+    def x_pass(who):
+        place = pl.ds(pl.multiple_of(who * rows, rows), rows)
+        return remote(
+            own_x.at[place], sib_x.at[place], pass_send.at[who], pass_recv.at[who], sibling
+        )
+
+    @pl.loop(1, 4)
+    def _(k):
+        x_out(k).start()
+
+    swaps = [
+        remote(
+            gate_ref.at[:, pl.ds(others, half)],
+            weight.at[pl.ds(feats, feats), pl.ds(0, half)],
+            swap_send.at[0],
+            swap_recv.at[0],
+            sibling,
+        ),
+        remote(
+            up_ref.at[:, pl.ds(others, half)],
+            weight.at[pl.ds(feats, feats), pl.ds(half, half)],
+            swap_send.at[1],
+            swap_recv.at[1],
+            sibling,
+        ),
+        remote(inv_gain_ref, sib_gain, swap_send.at[2], swap_recv.at[2], sibling),
+    ]
+    x_pass(c).start()
+    for swap in swaps:
+        swap.start()
+
+    @pl.loop(4, 16)
+    def _(k):
+        x_out(k).start()
+
+    for load in loads:
+        load.wait()
+    for swap in swaps:
+        swap.wait()
+
+    def sum_out(turn, k):
+        to = z_peer(k)
+        return remote(
+            part.at[turn, pl.ds(pl.multiple_of(to * rows, rows), rows)],
+            sums.at[turn, z],
+            sum_send.at[turn * 4 + k],
+            sum_recv.at[turn * 4 + z],
+            (c, to * 2 + core),
+        )
+
+    def sum_in(turn, k):
+        at = z_peer(k)
+        return remote(
+            part.at[turn, pl.ds(0, rows)],
+            sums.at[turn, at],
+            sum_send.at[turn * 4 + k],
+            sum_recv.at[turn * 4 + at],
+            (c, at * 2 + core),
+        )
+
+    def hid_out(turn, k):
+        return remote(
+            hidden.at[turn, core, z],
+            hidden.at[turn, core, z],
+            hid_send.at[turn * 4 + k],
+            hid_recv.at[turn * 4 + z],
+            (c, z_peer(k) * 2 + core),
+        )
+
+    def hid_in(turn, k):
+        at = z_peer(k)
+        return remote(
+            hidden.at[turn, core, at],
+            hidden.at[turn, core, at],
+            hid_send.at[turn * 4 + k],
+            hid_recv.at[turn * 4 + at],
+            (c, at * 2 + core),
+        )
+
+    def hid_pass(turn, at):
+        return remote(
+            hidden.at[turn, core, at],
+            hidden.at[turn, core, at],
+            hop_send.at[turn * 4 + at],
+            hop_recv.at[turn * 4 + at],
+            sibling,
+        )
+
+    def hid_passed(turn, at):
+        return remote(
+            hidden.at[turn, 1 - core, at],
+            hidden.at[turn, 1 - core, at],
+            hop_send.at[turn * 4 + at],
+            hop_recv.at[turn * 4 + at],
+            sibling,
+        )
+
+    def out_copy(who, slot):
+        return remote(
+            delta.at[pl.ds(pl.multiple_of(who * rows, rows), rows)],
+            deltas.at[slot],
+            out_send.at[who],
+            out_recv.at[slot],
+            (who, m),
+        )
+
+    def front(turn):
+        g = group_of(turn)
+
+        @pl.loop(0, 4)
+        def _(k):
+            who = g * 4 + lax.rem(y + 4 - k, 4)
+
+            @pl.when(who != c)
+            def _():
+                x_copy(who, (who, m)).wait_recv()
+                x_pass(who).start()
+
+        @pl.loop(0, 4)
+        def _(k):
+            who = g * 4 + lax.rem(y + 4 - k, 4)
+            x_pass(who).wait_recv()
+
+        place = pl.ds(pl.multiple_of(g * group, group), group)
+        mixed = own_x[place, :].astype(jnp.float32) * inv_gain_ref[0:1, :]
+        square = jnp.sum(mixed * mixed, axis=1, keepdims=True)
+        mixed = sib_x[place, :].astype(jnp.float32) * sib_gain[0:1, :]
+        square = square + jnp.sum(mixed * mixed, axis=1, keepdims=True)
+        square = jnp.broadcast_to(square, (group, 128))
+        coarse = square.astype(jnp.bfloat16)
+        fine = (square - coarse.astype(jnp.float32)).astype(jnp.bfloat16)
+        lane = lax.broadcasted_iota(jnp.int32, (group, 128), 1)
+        part[turn, :, pl.ds(both, 128)] = jnp.where(lane < 64, coarse, fine)
+
+        @pl.loop(0, both // 256)
+        def _(tile):
+            cols = pl.ds(pl.multiple_of(tile * 256, 256), 256)
+            total = jnp.dot(
+                own_x[place, :], weight[pl.ds(0, feats), cols], preferred_element_type=jnp.float32
+            )
+            total += jnp.dot(
+                sib_x[place, :],
+                weight[pl.ds(feats, feats), cols],
+                preferred_element_type=jnp.float32,
+            )
+            part[turn, :, cols] = total.astype(jnp.bfloat16)
+
+        for k in (2, 1, 3):
+            sum_out(turn, k).start()
+
+    def middle(turn):
+        total = part[turn, pl.ds(pl.multiple_of(z * rows, rows), rows), :].astype(jnp.float32)
+        for k in range(1, 4):
+            sum_in(turn, k).wait_recv()
+            total += sums[turn, z_peer(k)].astype(jnp.float32)
+        square = total[:, both : both + 1] + total[:, both + 64 : both + 65]
+        scale = lax.rsqrt(square * (1.0 / (8 * feats)) + EPS)
+        gate = total[:, :half] * scale
+        up = total[:, half:both] * scale
+        hidden[turn, core, z] = (gate / (1.0 + jnp.exp(-gate)) * up).astype(jnp.bfloat16)
+        for k in (2, 1, 3):
+            hid_out(turn, k).start()
+        hid_pass(turn, z).start()
+
+    def back(turn):
+        for k in range(1, 4):
+            hid_in(turn, k).wait_recv()
+            hid_pass(turn, z_peer(k)).start()
+        for k in range(4):
+            hid_passed(turn, z_peer(k)).wait_recv()
+        g = group_of(turn)
+        place = pl.ds(pl.multiple_of(g * group, group), group)
+
+        @pl.loop(0, feats // 256)
+        def _(tile):
+            cols = pl.ds(pl.multiple_of(tile * 256, 256), 256)
+            total = jnp.dot(
+                hidden[turn, 0].reshape(group, half),
+                down[pl.ds(0, half), cols],
+                preferred_element_type=jnp.float32,
+            )
+            total += jnp.dot(
+                hidden[turn, 1].reshape(group, half),
+                down[pl.ds(half, half), cols],
+                preferred_element_type=jnp.float32,
+            )
+            delta[place, cols] = total.astype(jnp.bfloat16)
+
+        @pl.loop(0, 4)
+        def _(k):
+            who = g * 4 + lax.rem(y + k, 4)
+
+            @pl.when(who != c)
+            def _():
+                out_copy(who, c).start()
+
+    @pl.loop(0, 6)
+    def _(step):
+        @pl.when(step < 4)
+        def _():
+            front(step)
+
+        @pl.when((step >= 1) & (step < 5))
+        def _():
+            middle(step - 1)
+
+        @pl.when(step >= 2)
+        def _():
+            back(step - 2)
+
+    out_ref[...] = delta[my_rows, :].astype(jnp.float32)
+
+    @pl.loop(1, 16)
+    def _(k):
+        who = peer(k)
+        out_copy(who, who).wait_recv()
+        out_ref[...] += deltas[who].astype(jnp.float32)
+
+    @pl.loop(1, 16)
+    def _(k):
+        x_out(k).wait_send()
+        out_copy(peer(k), c).wait_send()
+
+    @pl.loop(0, 16)
+    def _(who):
+        x_pass(who).wait_send()
+
+    @pl.loop(0, 4)
+    def _(turn):
+        for k in range(1, 4):
+            sum_out(turn, k).wait_send()
+            hid_out(turn, k).wait_send()
+        for k in range(4):
+            hid_pass(turn, z_peer(k)).wait_send()
+
+
+def feed_forward(scaled, inv_gain, gate_weight, up_weight, down_weight):
+    rows, feats = scaled.shape
+    cols = gate_weight.shape[1]
+    half = cols // 2
+    dma = pltpu.SemaphoreType.DMA
+    bf16 = jnp.bfloat16
+    vmem, anywhere = pl.BlockSpec(memory_space=pltpu.VMEM), pl.BlockSpec(memory_space=pl.ANY)
+    return pl.pallas_call(
+        mlp_kernel,
+        out_shape=jax.ShapeDtypeStruct((rows, feats), jnp.float32),
+        in_specs=[vmem, vmem, anywhere, anywhere, anywhere],
+        out_specs=vmem,
+        scratch_shapes=[
+            pltpu.VMEM((16 * rows, feats), bf16),
+            pltpu.VMEM((16 * rows, feats), bf16),
+            pltpu.VMEM((8, feats), jnp.float32),
+            pltpu.VMEM((2 * feats, cols), bf16),
+            pltpu.VMEM((cols, feats), bf16),
+            pltpu.VMEM((4, 4 * rows, cols + 128), bf16),
+            pltpu.VMEM((4, 4, rows, cols + 128), bf16),
+            pltpu.VMEM((4, 2, 4, rows, half), bf16),
+            pltpu.VMEM((16 * rows, feats), bf16),
+            pltpu.VMEM((16, rows, feats), bf16),
+            dma((3,)),
+            dma((3,)),
+            dma((3,)),
+        ]
+        + [dma((16,))] * 12,
+        compiler_params=pltpu.CompilerParams(
+            collective_id=3, has_side_effects=True, vmem_limit_bytes=56 * 2**20
+        ),
+        name="feed_forward",
+    )(scaled, inv_gain, gate_weight, up_weight, down_weight)
 
 
 def sent_to_all(shard, axis):
@@ -180,29 +565,14 @@
     )
     head_share = sent_and_summed(head_delta.astype(jnp.bfloat16), "mp", 1)
     mixed_share = local_rows.astype(jnp.float32) + head_share
-    square_sum = taken_together(jnp.sum(mixed_share * mixed_share, axis=1), "mp")
-    second_normed = (
-        mixed_share
-        * lax.rsqrt(square_sum / feature_total + 1e-05)[:, None]
-        * mlp_gain.astype(jnp.float32)
-    ).astype(jnp.bfloat16)
-    every_normed = collect(second_normed, "ctx", 0)
-    hidden_cols = gate_weight.shape[1]
-    gate_block = jnp.dot(every_normed, gate_weight, preferred_element_type=jnp.float32)
-    up_block = jnp.dot(every_normed, up_weight, preferred_element_type=jnp.float32)
-    gate_up = lax.psum_scatter(
-        jnp.concatenate([gate_block, up_block], axis=1).astype(jnp.bfloat16),
-        "mp",
-        scatter_dimension=0,
-        tiled=True,
-    ).astype(jnp.float32)
-    hidden = (jax.nn.silu(gate_up[:, :hidden_cols]) * gate_up[:, hidden_cols:]).astype(jnp.bfloat16)
-    mlp_partial = jnp.dot(
-        lax.all_gather(hidden, "mp", axis=0, tiled=True),
+    gain = mlp_gain.astype(jnp.float32)
+    mlp_share = feed_forward(
+        (mixed_share * gain).astype(jnp.bfloat16),
+        jnp.broadcast_to(1.0 / gain, (8, feature_cols)),
+        gate_weight,
+        up_weight,
         down_weight,
-        preferred_element_type=jnp.float32,
-    )
-    mlp_share = sent_and_summed(mlp_partial.astype(jnp.bfloat16), "ctx", 0)
+    )
     update = (router_score[:, None] * (head_share + mlp_share)).astype(jnp.bfloat16)
     returning = (
         jnp.zeros((slots_all, feature_cols), jnp.bfloat16)

time: 419 us -> 359 us (0.86)
  Pallas kernels: 0 us -> 112 us
  waiting for transfers between devices: 214 us -> 122 us
  blocking collectives: 76.8 us -> 24.4 us
  matrix products: 33 us -> 13.8 us
  other arithmetic: 20 us -> 10.1 us
    pallas_call x0 -> x1, Pallas kernels: none -> 112 us  [feed_forward(): pl.pallas_call(mlp_kernel, out_shape=jax.ShapeDtypeStruct((rows, feats),...]
    all_to_all x2 -> x0, blocking collectives: 52.5 us -> none  [the longest x1 33.2 us: sent_to_all(): lax.all_to_all(jnp.broadcast_to(shard[None], (count, *shard.shape)), axis...]
    reduce_scatter x1 -> x0, waiting for transfers between devices: 42.5 us -> none  [body(): lax.psum_scatter(jnp.concatenate([gate_block, up_block], axis=1).astype(j...]
    all_gather x1 -> x0, waiting for transfers between devices: 31.1 us -> none  [body(): lax.all_gather(hidden, 'mp', axis=0, tiled=True)]
    dot_general x3 -> x0, matrix products: 18 us -> none  [the longest x1 8.45 us: body(): jnp.dot(lax.all_gather(hidden, 'mp', axis=0, tiled=True), down_weight, pr...]
    all_to_all x1, waiting for transfers between devices: 29.3 us -> 14.1 us  [sent_and_summed(): lax.all_to_all(tiles, axis, split_axis=0, concat_axis=0, tiled=True)]
    all_to_all x1, starting transfers between devices: 4.43 us -> 12.6 us  [body(): lax.all_to_all(returning, 'ctx', split_axis=0, concat_axis=0, tiled=True)]
    concatenate x1 -> x0, other arithmetic: 5.57 us -> none  [body(): jnp.concatenate([gate_block, up_block], axis=1).astype(jnp.bfloat16)]
  transfers between devices with their start and end apart: 9 -> 6, of which waited for: 9 -> 6; matrix products, arithmetic and copies ran while one was open for 10% -> 11% of each run, Pallas kernels for 0% -> 0%
where the time goes in v1:
time: 359 us; the launch traced here: 358 us
  waiting for transfers between devices  122 us (34%)
  Pallas kernels  112 us (31%)
  local copies, waits for them, and re-layouts  31.6 us (9%)
  starting transfers between devices  30 us (8%)
  blocking collectives  24.4 us (7%)
  matrix products  13.8 us (4%)
  between operations  13.7 us (4%)
  other arithmetic  10.1 us (3%)
    pallas_call x1, Pallas kernels, feed_forward(): pl.pallas_call(mlp_kernel, out_shape=jax.ShapeDtypeStruct((rows, feats),...  112 us
    all_gather x1, waiting for transfers between devices, in_one_piece(): result, at, done = (lax.all_gather(both, axis, axis=dim, tiled=True), 0, [])  45.9 us
    all_gather x1, waiting for transfers between devices, body(): lax.all_gather(out_weight, 'ctx', axis=1, tiled=True)  28 us
    all_gather x1, blocking collectives, in_one_piece(): result, at, done = (lax.all_gather(both, axis, axis=dim, tiled=True), 0, [])  24.4 us
    dot_general x2, local copies, waits for them, and re-layouts, body(): query_sum = jnp.dot(normed, pieces[0], preferred_element_type=jnp.float32)  19.5 us
    all_to_all x1, waiting for transfers between devices, sent_to_all(): lax.all_to_all(jnp.broadcast_to(shard[None], (count, *shard.shape)), axis...  14.1 us
    all_to_all x1, waiting for transfers between devices, sent_and_summed(): lax.all_to_all(tiles, axis, split_axis=0, concat_axis=0, tiled=True)  14.1 us
    all_to_all x1, starting transfers between devices, body(): lax.all_to_all(returning, 'ctx', split_axis=0, concat_axis=0, tiled=True)  12.6 us
  transfers between devices with their start and end apart: 6, of which 6 were waited for; matrix products, arithmetic and copies ran while one was open for 11% of the time, Pallas kernels for 0%

profile of v1, /device:TPU:32, one launch (start us, length us, event | category | flops | bytes accessed | tf_op | source)
XLA Modules:
  0.0 357.8 jit_solution(8259683967611447640)
XLA Ops:
  6.5 2.2 pad_maximum_fusion
  8.8 0.7 all-gather.5.cloned.1.call-update
  11.0 2.4 scatter_custom_fusion
  13.4 0.8 gather_fusion
  14.4 0.8 broadcast_select_fusion
  15.2 7.0 %all-to-all-start = ((bf16[16,6,1024]{2,1,0:T(8,128)(2,1)}), bf16[16,6,1024]{2,1,0:T(8,128)(2,1)S(1)}, u32[]{:S(2)}, u32[]{:S(2)}) async-start(bf16[16,6,1024]{2,1,0:T(8,128)(2,1)} %broadcast_select_fusion), calls=%async_computation | async-start | bytes 524288 | tf_op jit(solution)/shard_map/all_to_all | solution.py:505
  22.5 10.9 %all-to-all-done = bf16[16,6,1024]{2,1,0:T(8,128)(2,1)S(1)} async-done(((bf16[16,6,1024]{2,1,0:T(8,128)(2,1)}), bf16[16,6,1024]{2,1,0:T(8,128)(2,1)S(1)}, u32[]{:S(2)}, u32[]{:S(2)}) %all-to-all-start) | async-done | bytes 196640 | tf_op jit(solution)/shard_map/all_to_all | solution.py:505
  33.5 0.7 gather_fusion.1
  34.2 1.1 broadcast_in_dim.151
  35.3 5.5 %all-to-all-start.1 = ((bf16[8,64,1024]{2,1,0:T(8,128)(2,1)}), bf16[8,64,1024]{2,1,0:T(8,128)(2,1)S(1)}, u32[]{:S(2)}, u32[]{:S(2)}) async-start(bf16[8,64,1024]{2,1,0:T(8,128)(2,1)} %broadcast_in_dim.151), calls=%async_computation.1 | async-start | bytes 2097152 | tf_op jit(solution)/shard_map/all_to_all | solution.py:396
  41.2 14.1 %all-to-all-done.1 = bf16[8,64,1024]{2,1,0:T(8,128)(2,1)S(1)} async-done(((bf16[8,64,1024]{2,1,0:T(8,128)(2,1)}), bf16[8,64,1024]{2,1,0:T(8,128)(2,1)S(1)}, u32[]{:S(2)}, u32[]{:S(2)}) %all-to-all-start.1) | async-done | bytes 1048608 | tf_op jit(solution)/shard_map/all_to_all | solution.py:396
  55.3 1.1 copy.31
  58.2 45.9 %all-gather.3.cloned.1.call-done = bf16[8192,768]{1,0:T(8,128)(2,1)} async-done(((bf16[512,768]{1,0:T(8,128)(2,1)}), bf16[8192,768]{1,0:T(8,128)(2,1)}) %all-gather.3.cloned.1.call-update) | async-done | bytes 12582928 | tf_op jit(solution)/shard_map/all_gather | solution.py:414
  104.0 7.4 %slice_bitcast_fusion = bf16[512,8192]{0,1:T(8,128)(2,1)} fusion(bf16[8192,768]{1,0:T(8,128)(2,1)} %all-gather.3.cloned.1.call-done), kind=kLoop, calls=%fused_computation.6 | loop fusion | bytes 16777216 | tf_op jit(solution)/shard_map/dot_general | solution.py:528
  111.4 12.1 %copy.27 = bf16[512,8192]{1,0:T(8,128)(2,1)} copy(bf16[512,8192]{0,1:T(8,128)(2,1)} %slice_bitcast_fusion) | data formatting | bytes 16777216 | tf_op jit(solution)/shard_map/dot_general | solution.py:528
  123.5 2.3 fusion.12
  126.1 2.7 fusion.15
  128.8 24.4 %all_gather.10 = bf16[1024,256]{1,0:T(8,128)(2,1)S(1)} all-gather(bf16[64,256]{1,0:T(8,128)(2,1)S(1)} %pad_maximum_fusion.1), channel_id=1, replica_groups=mesh['ctx'=16,'mp'=8] {'ctx'}, dimensions={0}, use_global_device_ids=true | all-gather | bytes 557056 | tf_op jit(solution)/shard_map/all_gather | solution.py:414
  153.2 2.7 fusion.61
  157.2 28.0 %all-gather.5.cloned.1.call-done = bf16[512,8192]{1,0:T(8,128)(2,1)} async-done(((bf16[512,512]{1,0:T(8,128)(2,1)}), bf16[512,8192]{1,0:T(8,128)(2,1)}) %all-gather.5.cloned.1.call-update) | async-done | bytes 8388624 | tf_op jit(solution)/shard_map/all_gather | solution.py:563
  185.2 4.9 %convolution_convert_fusion = bf16[64,8192]{1,0:T(8,128)(2,1)S(1)} fusion(bf16[512,8192]{1,0:T(8,128)(2,1)} %all-gather.5.cloned.1.call-done, bf16[8,8,4,128]{3,2,1,0:T(4,128)(2,1)S(1)} %bitcast.75), kind=kOutput, calls=%fused_computation.5 | convolution fusion | flops 537395200 | bytes 9502720 | tf_op jit(solution)/shard_map/dot_general | solution.py:561
  190.2 1.1 copy.38
  191.3 4.9 %all-to-all-start.2 = ((bf16[8,64,1024]{2,1,0:T(8,128)(2,1)}), bf16[8,64,1024]{2,1,0:T(8,128)(2,1)S(1)}, u32[]{:S(2)}, u32[]{:S(2)}) async-start(bf16[8,64,1024]{2,1,0:T(8,128)(2,1)} %bitcast.68), calls=%async_computation.2 | async-start | bytes 2097152 | tf_op jit(solution)/shard_map/all_to_all | solution.py:429
  196.6 14.1 %all-to-all-done.2 = bf16[8,64,1024]{2,1,0:T(8,128)(2,1)S(1)} async-done(((bf16[8,64,1024]{2,1,0:T(8,128)(2,1)}), bf16[8,64,1024]{2,1,0:T(8,128)(2,1)S(1)}, u32[]{:S(2)}, u32[]{:S(2)}) %all-to-all-start.2) | async-done | bytes 1048608 | tf_op jit(solution)/shard_map/all_to_all | solution.py:429
  210.9 0.7 multiply_convert_fusion.4.x_ref
  212.2 112.0 %feed_forward.1 = f32[64,1024]{1,0:T(8,128)} custom-call(bf16[64,1024]{1,0:T(8,128)(2,1)} %multiply_convert_fusion.4.x_ref, f32[8,1024]{1,0:T(8,128)} %broadcast_in_dim.156.inv_gain_ref, bf16[1024,1792]{1,0:T(8,128)(2,1)} %gate_ref.1, bf16[1024,1792]{1,0:T(8,128)(2,1)} %up_ref.1, bf16[1792,1024]{1,0:T(8,128)(2,1)} %down_ref.1), custom_call_target="tpu_custom_call" | custom-call | tf_op jit(solution)/shard_map/feed_forward/pallas_call | solution.py:366
  324.2 1.4 scatter_custom_fusion.1
  325.6 0.8 reshape.287
  326.4 12.6 %all-to-all-start.3 = ((bf16[16,6,1024]{2,1,0:T(8,128)(2,1)}), bf16[16,6,1024]{2,1,0:T(8,128)(2,1)S(1)}, u32[]{:S(2)}, u32[]{:S(2)}) async-start(bf16[16,6,1024]{2,1,0:T(8,128)(2,1)} %reshape.287), calls=%async_computation.3 | async-start | bytes 524288 | tf_op jit(solution)/shard_map/all_to_all | solution.py:583
  339.0 8.5 %all-to-all-done.3 = bf16[16,6,1024]{2,1,0:T(8,128)(2,1)S(1)} async-done(((bf16[16,6,1024]{2,1,0:T(8,128)(2,1)}), bf16[16,6,1024]{2,1,0:T(8,128)(2,1)S(1)}, u32[]{:S(2)}, u32[]{:S(2)}) %all-to-all-start.3) | async-done | bytes 196640 | tf_op jit(solution)/shard_map/all_to_all | solution.py:583
  347.5 2.1 gather_fusion.2
  349.6 1.4 add_convert_fusion
  (63 shorter events, 7.0 us)
Async XLA Ops:
  6.5 3.0 copy-start.6
  6.5 6.9 %copy-start.1 = (bf16[512,1024]{1,0:T(8,128)(2,1)S(1)}, bf16[512,1024]{1,0:T(8,128)(2,1)}, u32[]{:S(2)}) copy-start(bf16[512,1024]{1,0:T(8,128)(2,1)} %param.13) | copy-start | bytes 3145732
  6.5 97.5 %all-gather.3.cloned.1.call-start = ((), (), s32[]{:S(2)}) async-start(), calls=%async_computation.4 | async-start | bytes 13369344 | tf_op jit(solution)/shard_map/all_gather | solution.py:414
  8.8 13.5 %copy-start.7 = (s32[64]{0:T(128)S(1)}, s32[64]{0:T(128)}, u32[]{:S(2)}) copy-start(s32[64]{0:T(128)} %param.25) | copy-start | bytes 772
  8.8 176.5 %all-gather.5.cloned.1.call-start = ((), (), s32[]{:S(2)}) async-start(), calls=%async_computation.5 | async-start | bytes 8912896 | tf_op jit(solution)/shard_map/all_gather | solution.py:563
  15.2 18.2 %all-to-all-start = ((bf16[16,6,1024]{2,1,0:T(8,128)(2,1)}), bf16[16,6,1024]{2,1,0:T(8,128)(2,1)S(1)}, u32[]{:S(2)}, u32[]{:S(2)}) async-start(bf16[16,6,1024]{2,1,0:T(8,128)(2,1)} %broadcast_select_fusion), calls=%async_computation | async-start | bytes 524288 | tf_op jit(solution)/shard_map/all_to_all | solution.py:505
  33.5 7.3 %copy-start.3 = (bf16[8192]{0:T(1024)(128)(2,1)S(1)}, bf16[8192]{0:T(1024)(128)(2,1)}, u32[]{:S(2)}) copy-start(bf16[8192]{0:T(1024)(128)(2,1)} %param.14) | copy-start | bytes 49156
  35.3 20.0 %all-to-all-start.1 = ((bf16[8,64,1024]{2,1,0:T(8,128)(2,1)}), bf16[8,64,1024]{2,1,0:T(8,128)(2,1)S(1)}, u32[]{:S(2)}, u32[]{:S(2)}) async-start(bf16[8,64,1024]{2,1,0:T(8,128)(2,1)} %broadcast_in_dim.151), calls=%async_computation.1 | async-start | bytes 2097152 | tf_op jit(solution)/shard_map/all_to_all | solution.py:396
  111.4 12.1 %copy-start.2 = (bf16[8,8,8,1024]{3,2,0,1:T(8,128)(2,1)S(1)}, bf16[8,8,8,1024]{3,2,0,1:T(8,128)(2,1)}, u32[]{:S(2)}) copy-start(bf16[8,8,8,1024]{3,2,0,1:T(8,128)(2,1)} %copy.31) | copy-start | bytes 3145732
  123.5 29.7 %copy-start = (bf16[512,8192]{1,0:T(8,128)(2,1)S(1)}, bf16[512,8192]{1,0:T(8,128)(2,1)}, u32[]{:S(2)}) copy-start(bf16[512,8192]{1,0:T(8,128)(2,1)} %copy.27) | copy-start | bytes 25165828
  190.2 6.0 %copy-start.5 = (bf16[1024]{0:T(1024)(128)(2,1)S(1)}, bf16[1024]{0:T(1024)(128)(2,1)}, u32[]{:S(2)}) copy-start(bf16[1024]{0:T(1024)(128)(2,1)} %param.20) | copy-start | bytes 6148
  190.2 6.0 %copy-start.4 = (bf16[8192]{0:T(1024)(128)(2,1)S(1)}, bf16[8192]{0:T(1024)(128)(2,1)}, u32[]{:S(2)}) copy-start(bf16[8192]{0:T(1024)(128)(2,1)} %param.15) | copy-start | bytes 49156
  191.3 19.4 %all-to-all-start.2 = ((bf16[8,64,1024]{2,1,0:T(8,128)(2,1)}), bf16[8,64,1024]{2,1,0:T(8,128)(2,1)S(1)}, u32[]{:S(2)}, u32[]{:S(2)}) async-start(bf16[8,64,1024]{2,1,0:T(8,128)(2,1)} %bitcast.68), calls=%async_computation.2 | async-start | bytes 2097152 | tf_op jit(solution)/shard_map/all_to_all | solution.py:429
  326.4 21.0 %all-to-all-start.3 = ((bf16[16,6,1024]{2,1,0:T(8,128)(2,1)}), bf16[16,6,1024]{2,1,0:T(8,128)(2,1)S(1)}, u32[]{:S(2)}, u32[]{:S(2)}) async-start(bf16[16,6,1024]{2,1,0:T(8,128)(2,1)} %reshape.287), calls=%async_computation.3 | async-start | bytes 524288 | tf_op jit(solution)/shard_map/all_to_all | solution.py:583
Sparse Core Ops, SparseCore 0:
  9.5 94.4 all-gather.2
  106.1 79.0 all-gather.4

commit v2 on v1

--- a/solution.py
+++ b/solution.py
@@ -1,5 +1,3 @@
-import functools
-
 import jax
 import jax.numpy as jnp
 from jax import lax
@@ -9,6 +7,7 @@
 from jax.experimental.pallas import tpu as pltpu
 
 HEAD_DIM = 128
+BOX = 16
 MESH = pl.DeviceIdType.MESH
 EPS = 1e-05
 
@@ -26,6 +25,11 @@
 
 def mlp_kernel(
     x_ref,
+    share_ref,
+    score_ref,
+    take_ref,
+    send_ref,
+    tokens_ref,
     inv_gain_ref,
     gate_ref,
     up_ref,
@@ -41,6 +45,9 @@
     hidden,
     delta,
     deltas,
+    total_ref,
+    outbox,
+    inbox,
     load_sem,
     swap_send,
     swap_recv,
@@ -56,8 +63,12 @@
     hop_recv,
     out_send,
     out_recv,
+    box_send,
+    box_recv,
 ):
     rows, feats = x_ref.shape
+    slots = outbox.shape[0]
+    box = slots // 16
     half = gate_ref.shape[1] // 2
     both = 2 * half
     group = 4 * rows
@@ -330,18 +341,50 @@
         def _():
             back(step - 2)
 
-    out_ref[...] = delta[my_rows, :].astype(jnp.float32)
+    total_ref[...] = share_ref[...] + delta[my_rows, :].astype(jnp.float32)
 
     @pl.loop(1, 16)
     def _(k):
         who = peer(k)
         out_copy(who, who).wait_recv()
-        out_ref[...] += deltas[who].astype(jnp.float32)
+        total_ref[...] += deltas[who].astype(jnp.float32)
+
+    update = (score_ref[:, 0:1] * total_ref[...]).astype(jnp.bfloat16)
+    slot_at = lax.broadcasted_iota(jnp.int32, (slots, rows), 0)
+    give = jnp.where(slot_at == take_ref[0:1, :], 1.0, 0.0).astype(jnp.bfloat16)
+    outbox[...] = jnp.dot(give, update, preferred_element_type=jnp.float32).astype(jnp.bfloat16)
+
+    def box_of(who):
+        return pl.ds(pl.multiple_of(who * box, box), box)
+
+    def box_copy(who, slot):
+        return remote(
+            outbox.at[box_of(who)], inbox.at[box_of(slot)], box_send.at[who], box_recv.at[slot], (who, m)
+        )
+
+    @pl.loop(1, 16)
+    def _(k):
+        box_copy(peer(k), c).start()
+
+    inbox[box_of(c), :] = outbox[box_of(c), :]
+    slot_at = lax.broadcasted_iota(jnp.int32, (tokens_ref.shape[0], slots), 1)
+    back_to = jnp.where(slot_at == send_ref[:, 0:1], 1.0, 0.0).astype(jnp.bfloat16)
+
+    @pl.loop(1, 16)
+    def _(k):
+        box_copy(peer(k), peer(k)).wait_recv()
+
+    @pl.loop(0, feats // 256)
+    def _(tile):
+        cols = pl.ds(pl.multiple_of(tile * 256, 256), 256)
+        arrived = jnp.dot(back_to, inbox[:, cols], preferred_element_type=jnp.float32)
+        out_ref[:, cols] = (tokens_ref[:, cols].astype(jnp.float32) + arrived).astype(jnp.bfloat16)
 
     @pl.loop(1, 16)
     def _(k):
         x_out(k).wait_send()
         out_copy(peer(k), c).wait_send()
+        box_copy(peer(k), c).wait_send()
 
     @pl.loop(0, 16)
     def _(who):
@@ -356,7 +399,7 @@
             hid_pass(turn, z_peer(k)).wait_send()
 
 
-def feed_forward(scaled, inv_gain, gate_weight, up_weight, down_weight):
+def feed_forward(scaled, share, score, take, send, tokens, inv_gain, gate_weight, up_weight, down_weight):
     rows, feats = scaled.shape
     cols = gate_weight.shape[1]
     half = cols // 2
@@ -365,8 +408,8 @@
     vmem, anywhere = pl.BlockSpec(memory_space=pltpu.VMEM), pl.BlockSpec(memory_space=pl.ANY)
     return pl.pallas_call(
         mlp_kernel,
-        out_shape=jax.ShapeDtypeStruct((rows, feats), jnp.float32),
-        in_specs=[vmem, vmem, anywhere, anywhere, anywhere],
+        out_shape=jax.ShapeDtypeStruct(tokens.shape, bf16),
+        in_specs=[vmem] * 7 + [anywhere, anywhere, anywhere],
         out_specs=vmem,
         scratch_shapes=[
             pltpu.VMEM((16 * rows, feats), bf16),
@@ -379,78 +422,451 @@
             pltpu.VMEM((4, 2, 4, rows, half), bf16),
             pltpu.VMEM((16 * rows, feats), bf16),
             pltpu.VMEM((16, rows, feats), bf16),
+            pltpu.VMEM((rows, feats), jnp.float32),
+            pltpu.VMEM((16 * BOX, feats), bf16),
+            pltpu.VMEM((16 * BOX, feats), bf16),
             dma((3,)),
             dma((3,)),
             dma((3,)),
         ]
-        + [dma((16,))] * 12,
+        + [dma((16,))] * 14,
         compiler_params=pltpu.CompilerParams(
             collective_id=3, has_side_effects=True, vmem_limit_bytes=56 * 2**20
         ),
         name="feed_forward",
-    )(scaled, inv_gain, gate_weight, up_weight, down_weight)
-
-
-def sent_to_all(shard, axis):
-    count = lax.axis_size(axis)
-    return lax.all_to_all(
-        jnp.broadcast_to(shard[None], (count, *shard.shape)), axis, 0, 0, tiled=True
-    )
-
-
-def in_order(tiles, dim):
-    tiles = jnp.moveaxis(tiles, 0, dim)
-    dims = tiles.shape
-    return tiles.reshape(*dims[:dim], dims[dim] * dims[dim + 1], *dims[dim + 2 :])
-
-
-def collect(shard, axis, dim):
-    tiles = sent_to_all(shard, axis)
-    return in_order(tiles, dim)
-
-
-def in_one_piece(arrays, axis, dim, along):
-    both = jnp.concatenate(arrays, axis=along)
-    result, at, done = (lax.all_gather(both, axis, axis=dim, tiled=True), 0, [])
-    for a in arrays:
-        done.append(lax.slice_in_dim(result, at, at + a.shape[along], axis=along))
-        at += a.shape[along]
-    return tuple(done)
-
-
-def in_blocks(shard, dim, count):
-    dims = shard.shape
-    tiles = shard.reshape(*dims[:dim], count, dims[dim] // count, *dims[dim + 1 :])
-    return jnp.moveaxis(tiles, dim, 0)
-
-
-def sent_and_summed(shard, axis, dim):
-    tiles = in_blocks(shard, dim, lax.axis_size(axis))
-    arrived = lax.all_to_all(tiles, axis, split_axis=0, concat_axis=0, tiled=True)
-    return arrived.astype(jnp.float32).sum(axis=0)
-
-
-def taken_together(shard, axis):
-    everything = sent_to_all(shard, axis)
-    return jnp.sum(everything, axis=0)
-
-
-def rotate(values, positions):
-    half_dim = values.shape[-1] // 2
-    exponent = jnp.arange(half_dim, dtype=jnp.float32) * (2.0 / values.shape[-1])
-    frequency = 500000.0 ** (-exponent)
-    angles = positions.astype(jnp.float32)[:, None] * frequency[None, :]
-    cosine = jnp.cos(angles)[:, None, :]
-    sine_part = jnp.sin(angles)[:, None, :]
-    first_half = values[..., :half_dim]
-    second_half = values[..., half_dim:]
-    return jnp.concatenate(
-        [
-            first_half * cosine - second_half * sine_part,
-            second_half * cosine + first_half * sine_part,
-        ],
-        axis=-1,
-    )
+    )(scaled, share, score, take, send, tokens, inv_gain, gate_weight, up_weight, down_weight)
+
+
+def attend_kernel(
+    tokens_ref,
+    send_ref,
+    take_ref,
+    gain_ref,
+    router_ref,
+    query_ref,
+    key_ref,
+    value_ref,
+    out_weight_ref,
+    cosine_ref,
+    sine_ref,
+    mlp_gain_ref,
+    share_ref,
+    scaled_ref,
+    score_ref,
+    outbox,
+    inbox,
+    full,
+    normed,
+    blocks,
+    weight,
+    out_weight,
+    part,
+    parts,
+    key_value,
+    attended,
+    delta,
+    deltas,
+    load_sem,
+    box_send,
+    box_recv,
+    row_send,
+    row_recv,
+    hop_send,
+    hop_recv,
+    norm_send,
+    norm_recv,
+    part_send,
+    part_recv,
+    kv_send,
+    kv_recv,
+    att_send,
+    att_recv,
+    out_send,
+    out_recv,
+):
+    rows, feats = share_ref.shape
+    width = blocks.shape[1]
+    slots = outbox.shape[0]
+    box = slots // 16
+    group = 4 * rows
+    q_cols, kv_cols = query_ref.shape[1], key_ref.shape[1]
+    heads = q_cols // HEAD_DIM
+    c, m = lax.axis_index("ctx"), lax.axis_index("mp")
+    x, y = c // 4, c % 4
+    home = c // 2
+    z, core = m // 2, m % 2
+    sibling = (c, z * 2 + 1 - core)
+
+    def peer(step):
+        turn = step // 4
+        shift = turn + (turn // 2) * (1 - 2 * (turn % 2))
+        return lax.rem(x + 4 - shift, 4) * 4 + lax.rem(y + step % 4, 4)
+
+    def group_of(turn):
+        shift = turn + (turn // 2) * (1 - 2 * (turn % 2))
+        return lax.rem(x + shift, 4)
+
+    def rows_of(who, count=1):
+        return pl.ds(pl.multiple_of(who * (rows * count), rows), rows * count)
+
+    is_home = m == home
+    barrier = pltpu.get_barrier_semaphore()
+
+    @pl.loop(0, 16)
+    def _(k):
+        @pl.when(k > 0)
+        def _():
+            pl.semaphore_signal(barrier, inc=1, device_id=(peer(k), m), device_id_type=MESH)
+
+        @pl.when(jnp.logical_not(is_home & (k // 8 == c % 2) & (k % 8 == m)))
+        def _():
+            pl.semaphore_signal(
+                barrier, inc=1, device_id=(2 * m + k // 8, k % 8), device_id_type=MESH
+            )
+
+    for k in range(1, 4):
+        pl.semaphore_signal(
+            barrier,
+            inc=1,
+            device_id=(c, lax.rem(z + k, 4) * 2 + core),
+            device_id_type=MESH,
+        )
+    pl.semaphore_signal(barrier, inc=1, device_id=sibling, device_id_type=MESH)
+
+    loads = [
+        pltpu.make_async_copy(query_ref, weight.at[:, pl.ds(0, q_cols)], load_sem.at[0]),
+        pltpu.make_async_copy(key_ref, weight.at[:, pl.ds(q_cols, kv_cols)], load_sem.at[1]),
+        pltpu.make_async_copy(
+            value_ref, weight.at[:, pl.ds(q_cols + kv_cols, kv_cols)], load_sem.at[2]
+        ),
+        pltpu.make_async_copy(out_weight_ref, out_weight, load_sem.at[3]),
+    ]
+    for load in loads:
+        load.start()
+
+    slot_at = lax.broadcasted_iota(jnp.int32, (slots, tokens_ref.shape[0]), 0)
+    pick = jnp.where(slot_at == send_ref[0:1, :], 1.0, 0.0).astype(jnp.bfloat16)
+
+    @pl.loop(0, feats // 256)
+    def _(tile):
+        cols = pl.ds(pl.multiple_of(tile * 256, 256), 256)
+        outbox[:, cols] = jnp.dot(
+            pick, tokens_ref[:, cols], preferred_element_type=jnp.float32
+        ).astype(jnp.bfloat16)
+
+    def box_of(who):
+        return pl.ds(pl.multiple_of(who * box, box), box)
+
+    inbox[box_of(c), :] = outbox[box_of(c), :]
+    pl.semaphore_wait(barrier, jnp.where(is_home, 34, 35))
+
+    def box_copy(who, slot):
+        return remote(
+            outbox.at[box_of(who)], inbox.at[box_of(slot)], box_send.at[who], box_recv.at[slot], (who, m)
+        )
+
+    @pl.loop(1, 16)
+    def _(k):
+        box_copy(peer(k), c).start()
+
+    @pl.loop(1, 16)
+    def _(k):
+        box_copy(peer(k), peer(k)).wait_recv()
+
+    slot_at = lax.broadcasted_iota(jnp.int32, (rows, slots), 1)
+    take = jnp.where(slot_at == take_ref[:, 0:1], 1.0, 0.0).astype(jnp.bfloat16)
+    full[m] = jnp.dot(take, inbox[...], preferred_element_type=jnp.float32).astype(jnp.bfloat16)
+
+    def row_copy(k, who):
+        return remote(
+            full.at[who],
+            full.at[who],
+            row_send.at[k],
+            row_recv.at[who],
+            (c, lax.rem(z + k, 4) * 2 + core),
+        )
+
+    def hop(who):
+        return remote(full.at[who], full.at[who], hop_send.at[who], hop_recv.at[who], sibling)
+
+    def z_block(k):
+        return lax.rem(z + k, 4) * 2 + core
+
+    def z_sibling(k):
+        return lax.rem(z + k, 4) * 2 + 1 - core
+
+    for k in (2, 1, 3):
+        row_copy(k, m).start()
+    hop(m).start()
+    for k in (1, 3, 2):
+        row_copy(k, z_block(k)).wait_recv()
+        hop(z_block(k)).start()
+    for k in (0, 1, 3, 2):
+        hop(z_sibling(k)).wait_recv()
+
+    square, route = 0.0, 0.0
+    for at in range(8):
+        wide = full[at].astype(jnp.float32)
+        square += jnp.sum(wide * wide, axis=1, keepdims=True)
+        route += jnp.sum(wide * router_ref[at : at + 1, :], axis=1, keepdims=True)
+    scale = lax.rsqrt(square * (1.0 / (8 * feats)) + EPS)
+    score_ref[...] = jnp.broadcast_to(1.0 / (1.0 + jnp.exp(-route)), score_ref.shape)
+    for at in range(8):
+        wide = full[at].astype(jnp.float32) * scale * gain_ref[at : at + 1, :]
+        wide = wide.astype(jnp.bfloat16)
+        normed[2 * at] = wide[:, :width]
+        normed[2 * at + 1] = wide[:, width:]
+
+    def norm_copy(who, slot):
+        return remote(
+            normed.at[who], blocks.at[rows_of(slot)], norm_send.at[who], norm_recv.at[slot], (who, m)
+        )
+
+    @pl.loop(1, 16)
+    def _(k):
+        norm_copy(peer(k), c).start()
+
+    blocks[rows_of(c), :] = normed[c]
+    for load in loads:
+        load.wait()
+
+    def part_copy(who, slot):
+        return remote(
+            part.at[rows_of(who)], parts.at[slot], part_send.at[who], part_recv.at[slot], (who, m)
+        )
+
+    @pl.loop(0, 4)
+    def _(turn):
+        g = group_of(turn)
+
+        @pl.loop(0, 4)
+        def _(k):
+            who = g * 4 + k
+
+            @pl.when(who != c)
+            def _():
+                norm_copy(who, who).wait_recv()
+
+        here = rows_of(g, 4)
+        part[here, :] = jnp.dot(
+            blocks[here, :], weight[...], preferred_element_type=jnp.float32
+        ).astype(jnp.bfloat16)
+
+        @pl.loop(0, 4)
+        def _(k):
+            who = g * 4 + lax.rem(y + k, 4)
+
+            @pl.when(who != c)
+            def _():
+                part_copy(who, c).start()
+
+    for at in range(0, weight.shape[1], HEAD_DIM):
+        total_at = part[rows_of(c), at : at + HEAD_DIM]
+        share_ref[:, at : at + HEAD_DIM] = total_at.astype(jnp.float32)
+
+    @pl.loop(1, 16)
+    def _(k):
+        who = peer(k)
+        part_copy(who, who).wait_recv()
+        share_ref[:, 0 : weight.shape[1]] += parts[who].astype(jnp.float32)
+
+    def turned(at):
+        head = share_ref[:, at : at + HEAD_DIM]
+        swapped = pltpu.roll(head, HEAD_DIM // 2, 1)
+        return (head * cosine_ref[...] + swapped * sine_ref[...]).astype(jnp.bfloat16)
+
+    mine = rows_of(c)
+    key_value[mine, 0:HEAD_DIM] = turned(q_cols)
+    at = q_cols + kv_cols
+    key_value[mine, HEAD_DIM : 2 * HEAD_DIM] = share_ref[:, at : at + HEAD_DIM].astype(jnp.bfloat16)
+
+    def kv_copy(k, who):
+        return remote(
+            key_value.at[rows_of(who)],
+            key_value.at[rows_of(who)],
+            kv_send.at[k],
+            kv_recv.at[who],
+            (peer(k), m),
+        )
+
+    @pl.loop(1, 16)
+    def _(k):
+        kv_copy(k, c).start()
+
+    queries = jnp.concatenate([turned(h * HEAD_DIM) for h in range(heads)], axis=0)
+
+    @pl.loop(1, 16)
+    def _(k):
+        kv_copy(k, peer(k)).wait_recv()
+
+    keys = 16 * rows
+    scores = lax.dot_general(
+        queries,
+        key_value[:, 0:HEAD_DIM],
+        (((1,), (1,)), ((), ())),
+        preferred_element_type=jnp.float32,
+    ) * (HEAD_DIM ** (-0.5))
+    query_at = lax.broadcasted_iota(jnp.int32, (heads * rows, keys), 0) % rows * 16 + c
+    key_at = lax.broadcasted_iota(jnp.int32, (heads * rows, keys), 1)
+    allowed = key_at % rows * 16 + key_at // rows <= query_at
+    scores = jnp.where(allowed, scores, -1e30)
+    weights = jnp.exp(scores - jnp.max(scores, axis=1, keepdims=True))
+    weights = jnp.where(allowed, weights, 0.0)
+    total = jnp.sum(weights, axis=1, keepdims=True)
+    mixed = (
+        jnp.dot(
+            weights.astype(jnp.bfloat16),
+            key_value[:, HEAD_DIM : 2 * HEAD_DIM],
+            preferred_element_type=jnp.float32,
+        )
+        / total
+    ).astype(jnp.bfloat16)
+    for h in range(heads):
+        attended[mine, h * HEAD_DIM : (h + 1) * HEAD_DIM] = mixed[h * rows : (h + 1) * rows]
+
+    def att_copy(k, who):
+        return remote(
+            attended.at[rows_of(who)],
+            attended.at[rows_of(who)],
+            att_send.at[k],
+            att_recv.at[who],
+            (peer(k), m),
+        )
+
+    @pl.loop(1, 16)
+    def _(k):
+        att_copy(k, c).start()
+
+    my_slot = (c % 2) * 8 + m
+
+    def out_copy(who):
+        return remote(
+            delta.at[rows_of(who)],
+            deltas.at[my_slot],
+            out_send.at[who],
+            out_recv.at[my_slot],
+            (who, home),
+        )
+
+    def out_in(slot):
+        return remote(
+            delta.at[pl.ds(0, rows)],
+            deltas.at[slot],
+            out_send.at[slot],
+            out_recv.at[slot],
+            (2 * m + slot // 8, slot % 8),
+        )
+
+    @pl.loop(0, 4)
+    def _(turn):
+        g = group_of(turn)
+
+        @pl.loop(0, 4)
+        def _(k):
+            who = g * 4 + lax.rem(y + 4 - k, 4)
+
+            @pl.when(who != c)
+            def _():
+                step = turn * 4 + k
+                att_copy(step, who).wait_recv()
+
+        here = rows_of(g, 4)
+        delta[here, :] = jnp.dot(
+            attended[here, :], out_weight[...], preferred_element_type=jnp.float32
+        ).astype(jnp.bfloat16)
+
+        @pl.loop(0, 4)
+        def _(k):
+            who = g * 4 + lax.rem(y + k, 4)
+
+            @pl.when(jnp.logical_not(is_home & (who == c)))
+            def _():
+                out_copy(who).start()
+
+    @pl.when(is_home)
+    def _():
+        deltas[my_slot] = delta[mine, :]
+
+    share_ref[...] = jnp.zeros_like(share_ref)
+
+    for side in range(2):
+
+        @pl.loop(0, 8)
+        def _(k):
+            slot = side * 8 + lax.rem(k + m, 8)
+
+            @pl.when(jnp.logical_not(is_home & (slot == my_slot)))
+            def _():
+                out_in(slot).wait_recv()
+
+            share_ref[:, side * width : (side + 1) * width] += deltas[slot].astype(jnp.float32)
+
+    mixed = full[m].astype(jnp.float32) + share_ref[...]
+    scaled_ref[...] = (mixed * mlp_gain_ref[0:1, :]).astype(jnp.bfloat16)
+
+    for k in range(1, 4):
+        row_copy(k, m).wait_send()
+    for k in range(4):
+        hop(z_block(k)).wait_send()
+
+    @pl.loop(0, 16)
+    def _(k):
+        @pl.when(jnp.logical_not(is_home & (k == c)))
+        def _():
+            out_copy(k).wait_send()
+
+        @pl.when(k != c)
+        def _():
+            box_copy(k, c).wait_send()
+            norm_copy(k, c).wait_send()
+            part_copy(k, c).wait_send()
+
+        @pl.when(k > 0)
+        def _():
+            kv_copy(k, c).wait_send()
+            att_copy(k, c).wait_send()
+
+
+def attend(tokens, send, take, gain, router, query, key, value, out_weight, cosine, sine, mlp_gain):
+    count, slots = take.shape[0], 16 * BOX
+    feats = tokens.shape[1]
+    width = query.shape[0]
+    cols = query.shape[1] + key.shape[1] + value.shape[1]
+    out_cols = out_weight.shape[1]
+    dma = pltpu.SemaphoreType.DMA
+    bf16 = jnp.bfloat16
+    vmem, anywhere = pl.BlockSpec(memory_space=pltpu.VMEM), pl.BlockSpec(memory_space=pl.ANY)
+    return pl.pallas_call(
+        attend_kernel,
+        out_shape=(
+            jax.ShapeDtypeStruct((count, feats), jnp.float32),
+            jax.ShapeDtypeStruct((count, feats), bf16),
+            jax.ShapeDtypeStruct((count, 128), jnp.float32),
+        ),
+        in_specs=[vmem] * 5 + [anywhere] * 4 + [vmem] * 3,
+        out_specs=(vmem, vmem, vmem),
+        scratch_shapes=[
+            pltpu.VMEM((slots, feats), bf16),
+            pltpu.VMEM((slots, feats), bf16),
+            pltpu.VMEM((8, count, feats), bf16),
+            pltpu.VMEM((16, count, width), bf16),
+            pltpu.VMEM((16 * count, width), bf16),
+            pltpu.VMEM((width, cols), bf16),
+            pltpu.VMEM(out_weight.shape, bf16),
+            pltpu.VMEM((16 * count, cols), bf16),
+            pltpu.VMEM((16, count, cols), bf16),
+            pltpu.VMEM((16 * count, 2 * HEAD_DIM), bf16),
+            pltpu.VMEM((16 * count, query.shape[1]), bf16),
+            pltpu.VMEM((16 * count, out_cols), bf16),
+            pltpu.VMEM((16, count, out_cols), bf16),
+            dma((4,)),
+        ]
+        + [dma((16,))] * 16,
+        compiler_params=pltpu.CompilerParams(
+            collective_id=2, has_side_effects=True, vmem_limit_bytes=48 * 2**20
+        ),
+        name="attend",
+    )(tokens, send, take, gain, router, query, key, value, out_weight, cosine, sine, mlp_gain)
 
 
 def body(
@@ -469,20 +885,11 @@
     kept_pos,
 ):
     ctx_count = lax.axis_size("ctx")
-    mp_count = lax.axis_size("mp")
-    my_index = lax.axis_index("ctx")
     tok_dev = tokens.shape[0]
     kept_dev = kept_pos.shape[0]
     feature_cols = tokens.shape[1]
-    feature_total = feature_cols * mp_count
-    capacity = (3 * kept_dev // 2 + ctx_count - 1) // ctx_count
+    capacity = BOX
     slots_all = ctx_count * capacity
-    head_dim = HEAD_DIM
-    query_cols = query_weight.shape[1]
-    key_cols = key_weight.shape[1]
-    kv_local = key_cols // head_dim
-    q_local = query_cols // head_dim
-    group_size = q_local // kv_local
     peer_ids = jnp.arange(ctx_count, dtype=jnp.int32)
     is_kept = destination >= 0
     owner_ids = destination // kept_dev
@@ -497,14 +904,6 @@
         - jnp.sum(jnp.where(owner_match, first_slots[None, :], 0), axis=1)
     )
     send_index = jnp.where(is_kept, send_index, slots_all)
-    token_ids = jnp.arange(tok_dev, dtype=jnp.int32)
-    picked = jnp.full((slots_all,), tok_dev, jnp.int32).at[send_index].set(token_ids, mode="drop")
-    outgoing = jnp.take(tokens, picked, axis=0, mode="fill", fill_value=0).reshape(
-        ctx_count, capacity, feature_cols
-    )
-    incoming = lax.all_to_all(outgoing, "ctx", split_axis=0, concat_axis=0, tiled=True).reshape(
-        slots_all, feature_cols
-    )
     slot_range = jnp.arange(kept_dev, dtype=jnp.int32)
     source_ids = kept_pos // tok_dev
     source_match = source_ids[:, None] == peer_ids[None, :]
@@ -514,77 +913,37 @@
         + slot_range
         - jnp.sum(jnp.where(source_match, first_from[None, :], 0), axis=1)
     )
-    local_rows = incoming[recv_index]
-    full_rows = collect(local_rows, "mp", 1)
-    raw_rows = full_rows.astype(jnp.float32)
-    mean_square = jnp.mean(raw_rows * raw_rows, axis=-1, keepdims=True)
-    normed = (raw_rows * lax.rsqrt(mean_square + 1e-05) * norm_gain.astype(jnp.float32)).astype(
-        jnp.bfloat16
+    half_dim = HEAD_DIM // 2
+    exponent = jnp.arange(half_dim, dtype=jnp.float32) * (2.0 / HEAD_DIM)
+    angles = kept_pos.astype(jnp.float32)[:, None] * (500000.0 ** (-exponent))[None, :]
+    cosine, sine = jnp.cos(angles), jnp.sin(angles)
+    later_gain = mlp_gain.astype(jnp.float32)
+    head_share, scaled, score = attend(
+        tokens,
+        jnp.broadcast_to(send_index, (8, tok_dev)),
+        jnp.broadcast_to(recv_index[:, None], (kept_dev, 128)),
+        norm_gain.astype(jnp.float32).reshape(8, feature_cols),
+        router_weight.astype(jnp.float32).reshape(8, feature_cols),
+        query_weight,
+        key_weight,
+        value_weight,
+        out_weight,
+        jnp.concatenate([cosine, cosine], axis=1),
+        jnp.concatenate([-sine, sine], axis=1),
+        jnp.broadcast_to(later_gain, (8, feature_cols)),
     )
-    router_score = jax.nn.sigmoid(
-        jnp.dot(full_rows, router_weight, preferred_element_type=jnp.float32)
-    )
-    pieces = in_one_piece((query_weight, key_weight, value_weight), "ctx", 0, 1)
-    query_sum = jnp.dot(normed, pieces[0], preferred_element_type=jnp.float32)
-    key_sum = jnp.dot(normed, pieces[1], preferred_element_type=jnp.float32)
-    value_sum = jnp.dot(normed, pieces[2], preferred_element_type=jnp.float32)
-    queries = rotate(query_sum.reshape(kept_dev, q_local, head_dim), kept_pos).astype(jnp.bfloat16)
-    queries = queries.reshape(kept_dev, kv_local, group_size, head_dim)
-    key_rows = (
-        rotate(key_sum.reshape(kept_dev, kv_local, head_dim), kept_pos)
-        .astype(jnp.bfloat16)
-        .reshape(kept_dev, key_cols)
-    )
-    value_rows = value_sum.astype(jnp.bfloat16)
-    query_order = slot_range * ctx_count + my_index
-    softmax_scale = head_dim ** (-0.5)
-    running_max = jnp.full((kept_dev, kv_local, group_size), -1e30, jnp.float32)
-    key_piece, value_piece = in_one_piece((key_rows, value_rows), "ctx", 0, 1)
-    piece_rows = key_piece.shape[0]
-    key_piece = key_piece.reshape(piece_rows, kv_local, head_dim)
-    value_piece = value_piece.reshape(piece_rows, kv_local, head_dim).astype(jnp.float32)
-    row_ids = jnp.arange(piece_rows, dtype=jnp.int32)
-    key_order = row_ids % kept_dev * ctx_count + row_ids // kept_dev
-    allowed = (key_order[None, :] <= query_order[:, None])[:, None, None, :]
-    scores = (
-        jnp.einsum("qhgd,khd->qhgk", queries, key_piece, preferred_element_type=jnp.float32)
-        * softmax_scale
-    )
-    scores = jnp.where(allowed, scores, -1e30)
-    new_max = jnp.maximum(running_max, jnp.max(scores, axis=-1))
-    weights = jnp.where(allowed, jnp.exp(scores - new_max[..., None]), 0.0)
-    running_sum = jnp.sum(weights, axis=-1)
-    weighted = jnp.einsum("qhgk,khd->qhgd", weights, value_piece)
-    attended = (
-        (weighted / running_sum[..., None]).reshape(kept_dev, query_cols).astype(jnp.bfloat16)
-    )
-    head_delta = jnp.dot(
-        attended,
-        lax.all_gather(out_weight, "ctx", axis=1, tiled=True),
-        preferred_element_type=jnp.float32,
-    )
-    head_share = sent_and_summed(head_delta.astype(jnp.bfloat16), "mp", 1)
-    mixed_share = local_rows.astype(jnp.float32) + head_share
-    gain = mlp_gain.astype(jnp.float32)
-    mlp_share = feed_forward(
-        (mixed_share * gain).astype(jnp.bfloat16),
-        jnp.broadcast_to(1.0 / gain, (8, feature_cols)),
+    return feed_forward(
+        scaled,
+        head_share,
+        score,
+        jnp.broadcast_to(recv_index, (8, kept_dev)),
+        jnp.broadcast_to(send_index[:, None], (tok_dev, 128)),
+        tokens,
+        jnp.broadcast_to(1.0 / later_gain, (8, feature_cols)),
         gate_weight,
         up_weight,
         down_weight,
     )
-    update = (router_score[:, None] * (head_share + mlp_share)).astype(jnp.bfloat16)
-    returning = (
-        jnp.zeros((slots_all, feature_cols), jnp.bfloat16)
-        .at[recv_index]
-        .set(update)
-        .reshape(ctx_count, capacity, feature_cols)
-    )
-    returned = lax.all_to_all(returning, "ctx", split_axis=0, concat_axis=0, tiled=True).reshape(
-        slots_all, feature_cols
-    )
-    arriving = jnp.take(returned, send_index, axis=0, mode="fill", fill_value=0)
-    return (tokens.astype(jnp.float32) + arriving.astype(jnp.float32)).astype(jnp.bfloat16)
 
 
 def solution(mesh):

time: 359 us -> 263 us (0.73)
  the two profiles are of different devices: /device:TPU:32 before, /device:TPU:6 now
where the time goes in v2:
time: 263 us; the launch traced here: 262 us
  Pallas kernels  244 us (93%)
  local copies, waits for them, and re-layouts  13.6 us (5%)
  other arithmetic  4.7 us (2%)
    pallas_call x1, Pallas kernels, feed_forward(): pl.pallas_call(mlp_kernel, out_shape=jax.ShapeDtypeStruct(tokens.shape, b...  141 us
    pallas_call x1, Pallas kernels, attend(): pl.pallas_call(attend_kernel, out_shape=(jax.ShapeDtypeStruct((count, fea...  103 us
    unnamed x17, local copies, waits for them, and re-layouts  9.33 us

profile of v2, /device:TPU:6, one launch (start us, length us, event | category | flops | bytes accessed | tf_op | source)
XLA Modules:
  0.0 262.3 jit_solution(16184136983533180832)
XLA Ops:
  0.0 0.7 fusion.2
  0.8 0.1 select_reduce_fusion.2
  0.9 0.1 select_reduce_fusion.1
  1.0 1.3 add_select_fusion.1
  2.3 0.7 and_select_fusion.1
  3.0 0.1 select_reduce_fusion
  3.0 0.7 subtract_select_fusion
  3.7 0.6 broadcast_in_dim.87.take_ref
  4.3 0.7 broadcast_divide_fusion
  5.0 0.6 broadcast_in_dim.89.inv_gain_ref
  5.6 0.1 broadcast_in_dim.85.take_ref
  5.7 0.7 reshape.47.gain_ref
  6.4 0.7 reshape.49.router_ref
  7.2 0.7 broadcast_in_dim.86.mlp_gain_ref
  7.9 0.2 fusion
  8.1 0.1 pad_maximum_fusion
  8.2 0.0 copy-start
  8.2 1.2 copy-done
  9.4 0.0 copy-start.1
  9.4 1.0 copy-done.1
  10.4 0.0 copy-start.2
  10.4 1.0 copy-done.2
  11.5 0.9 copy-done.5
  12.4 0.9 copy-done.6
  13.3 103.3 %attend.1 = (f32[64,1024]{1,0:T(8,128)S(1)}, bf16[64,1024]{1,0:T(8,128)(2,1)S(1)}, f32[64,128]{1,0:T(8,128)S(1)}) custom-call(bf16[512,1024]{1,0:T(8,128)(2,1)S(1)} %copy-done, s32[8,512]{1,0:T(8,128)S(1)} %broadcast_in_dim.80.send_ref, s32[64,128]{1,0:T(8,128)S(1)} %broadcast_in_dim.85.take_ref, f32[8,1024]{1,0:T(8,128)S(1)} %reshape.47.gain_ref, ...), custom_call_target="tpu_custom_call" | custom-call | tf_op jit(solution)/shard_map/attend/pallas_call | solution.py:839
  116.6 0.0 copy-start.3
  116.6 0.7 copy-done.3
  117.3 0.6 copy-done.4
  118.0 0.6 copy-done.7
  118.6 0.9 broadcast_in_dim.88.send_ref
  119.4 140.6 %feed_forward.1 = bf16[512,1024]{1,0:T(8,128)(2,1)} custom-call(bf16[64,1024]{1,0:T(8,128)(2,1)} %copy-done.4, f32[64,1024]{1,0:T(8,128)} %copy-done.3, f32[64,128]{1,0:T(8,128)} %copy-done.7, s32[8,64]{1,0:T(8,128)} %broadcast_in_dim.87.take_ref, s32[512,128]{1,0:T(8,128)} %broadcast_in_dim.88.send_ref, bf16[512,1024]{1,0:T(8,128)(2,1)} %tokens_ref.3, ...), custom_call_target="tpu_custom_call" | custom-call | tf_op jit(solution)/shard_map/feed_forward/pallas_call | solution.py:409
  260.0 2.3 copy.15
  (7 shorter events, 0.0 us)
Async XLA Ops:
  8.2 1.2 copy-start
  9.4 1.0 copy-start.1
  10.4 1.0 copy-start.2
  11.5 0.9 copy-start.5
  12.4 0.9 copy-start.6
  116.6 0.7 copy-start.3
  117.3 0.7 copy-start.4
  118.0 0.6 copy-start.7

commit v3 on v2

--- a/solution.py
+++ b/solution.py
@@ -9,7 +9,21 @@
 HEAD_DIM = 128
 BOX = 16
 MESH = pl.DeviceIdType.MESH
+OFFSETS = (
+    (0, 0), (0, 1), (1, 0), (0, 3), (3, 0), (1, 1), (3, 3), (1, 3),
+    (3, 1), (0, 2), (2, 0), (1, 2), (2, 1), (3, 2), (2, 3), (2, 2),
+)
 EPS = 1e-05
+
+
+def ahead(c, k):
+    dx, dy = OFFSETS[k]
+    return lax.rem(c // 4 + dx, 4) * 4 + lax.rem(c % 4 + dy, 4)
+
+
+def behind(c, k):
+    dx, dy = OFFSETS[k]
+    return lax.rem(c // 4 + 4 - dx, 4) * 4 + lax.rem(c % 4 + 4 - dy, 4)
 
 
 def remote(source, target, sent, landed, device):
@@ -33,6 +47,8 @@
     inv_gain_ref,
     gate_ref,
     up_ref,
+    gate_half_ref,
+    up_half_ref,
     down_ref,
     out_ref,
     own_x,
@@ -41,6 +57,8 @@
     weight,
     down,
     part,
+    relayed,
+    joined,
     sums,
     hidden,
     delta,
@@ -55,10 +73,16 @@
     x_recv,
     pass_send,
     pass_recv,
+    far_send,
+    far_recv,
     sum_send,
     sum_recv,
+    join_send,
+    join_recv,
     hid_send,
     hid_recv,
+    lap_send,
+    lap_recv,
     hop_send,
     hop_recv,
     out_send,
@@ -77,32 +101,21 @@
     z, core = m // 2, m % 2
     sibling = (c, z * 2 + 1 - core)
 
-    def peer(step):
-        turn = step // 4
-        shift = turn + (turn // 2) * (1 - 2 * (turn % 2))
-        return lax.rem(x + 4 - shift, 4) * 4 + lax.rem(y + step % 4, 4)
-
     def z_peer(step):
         return lax.rem(z + step, 4)
 
-    def group_of(turn):
-        shift = turn + (turn // 2) * (1 - 2 * (turn % 2))
-        return lax.rem(x + shift, 4)
-
     barrier = pltpu.get_barrier_semaphore()
 
-    @pl.loop(1, 16)
-    def _(k):
-        pl.semaphore_signal(barrier, inc=1, device_id=(peer(k), m), device_id_type=MESH)
-
-    for k in range(1, 4):
+    for k in range(1, 16):
+        pl.semaphore_signal(barrier, inc=1, device_id=(ahead(c, k), m), device_id_type=MESH)
+
+    for k in (1, 3):
         pl.semaphore_signal(
             barrier, inc=1, device_id=(c, z_peer(k) * 2 + core), device_id_type=MESH
         )
     pl.semaphore_signal(barrier, inc=1, device_id=sibling, device_id_type=MESH)
 
     mine = pl.multiple_of(core * half, 128)
-    others = pl.multiple_of((1 - core) * half, 128)
     loads = [
         pltpu.make_async_copy(
             gate_ref.at[:, pl.ds(mine, half)],
@@ -114,22 +127,26 @@
             weight.at[pl.ds(0, feats), pl.ds(half, half)],
             load_sem.at[1],
         ),
-        pltpu.make_async_copy(down_ref, down, load_sem.at[2]),
+        pltpu.make_async_copy(
+            gate_half_ref, weight.at[pl.ds(feats, feats), pl.ds(0, half)], load_sem.at[2]
+        ),
+        pltpu.make_async_copy(
+            up_half_ref, weight.at[pl.ds(feats, feats), pl.ds(half, half)], load_sem.at[3]
+        ),
+        pltpu.make_async_copy(down_ref, down, load_sem.at[4]),
     ]
     for load in loads:
         load.start()
-    my_rows = pl.ds(pl.multiple_of(c * rows, rows), rows)
-    own_x[my_rows, :] = x_ref[...]
-    pl.semaphore_wait(barrier, 19)
-
-    def x_copy(who, device):
-        place = pl.ds(pl.multiple_of(who * rows, rows), rows)
-        return remote(own_x.at[place], own_x.at[place], x_send.at[who], x_recv.at[who], device)
-
-    def x_out(k):
-        return remote(
-            own_x.at[my_rows], own_x.at[my_rows], x_send.at[k], x_recv.at[c], (peer(k), m)
-        )
+    own_x[0:rows, :] = x_ref[...]
+    pl.semaphore_wait(barrier, 18)
+
+    def x_copy(k):
+        place = pl.ds(k * rows, rows)
+        return remote(x_ref, own_x.at[place], x_send.at[k], x_recv.at[k], (behind(c, k), m))
+
+    def x_in(slot):
+        place = pl.ds(pl.multiple_of(slot * rows, rows), rows)
+        return remote(x_ref, own_x.at[place], x_send.at[slot], x_recv.at[slot], sibling)
 
     def x_pass(who):
         place = pl.ds(pl.multiple_of(who * rows, rows), rows)
@@ -137,78 +154,67 @@
             own_x.at[place], sib_x.at[place], pass_send.at[who], pass_recv.at[who], sibling
         )
 
-    @pl.loop(1, 4)
-    def _(k):
-        x_out(k).start()
-
-    swaps = [
-        remote(
-            gate_ref.at[:, pl.ds(others, half)],
-            weight.at[pl.ds(feats, feats), pl.ds(0, half)],
-            swap_send.at[0],
-            swap_recv.at[0],
-            sibling,
-        ),
-        remote(
-            up_ref.at[:, pl.ds(others, half)],
-            weight.at[pl.ds(feats, feats), pl.ds(half, half)],
-            swap_send.at[1],
-            swap_recv.at[1],
-            sibling,
-        ),
-        remote(inv_gain_ref, sib_gain, swap_send.at[2], swap_recv.at[2], sibling),
-    ]
-    x_pass(c).start()
-    for swap in swaps:
-        swap.start()
-
-    @pl.loop(4, 16)
-    def _(k):
-        x_out(k).start()
-
-    for load in loads:
-        load.wait()
-    for swap in swaps:
-        swap.wait()
-
-    def sum_out(turn, k):
-        to = z_peer(k)
-        return remote(
-            part.at[turn, pl.ds(pl.multiple_of(to * rows, rows), rows)],
-            sums.at[turn, z],
-            sum_send.at[turn * 4 + k],
-            sum_recv.at[turn * 4 + z],
-            (c, to * 2 + core),
-        )
-
-    def sum_in(turn, k):
-        at = z_peer(k)
-        return remote(
-            part.at[turn, pl.ds(0, rows)],
-            sums.at[turn, at],
-            sum_send.at[turn * 4 + k],
-            sum_recv.at[turn * 4 + at],
-            (c, at * 2 + core),
-        )
-
-    def hid_out(turn, k):
-        return remote(
-            hidden.at[turn, core, z],
-            hidden.at[turn, core, z],
-            hid_send.at[turn * 4 + k],
-            hid_recv.at[turn * 4 + z],
-            (c, z_peer(k) * 2 + core),
-        )
-
-    def hid_in(turn, k):
-        at = z_peer(k)
-        return remote(
-            hidden.at[turn, core, at],
-            hidden.at[turn, core, at],
-            hid_send.at[turn * 4 + k],
-            hid_recv.at[turn * 4 + at],
-            (c, at * 2 + core),
-        )
+    for k in range(1, 4):
+        x_copy(k).start()
+    gain_swap = remote(inv_gain_ref, sib_gain, swap_send.at[0], swap_recv.at[0], sibling)
+    x_pass(0).start()
+    gain_swap.start()
+
+    short = rows // 2
+
+    def near(way):
+        return z_peer(1 + 2 * way)
+
+    def chip(way):
+        return (c, near(way) * 2 + core)
+
+    def piece(turn, to, side):
+        return part.at[turn, pl.ds(pl.multiple_of(to * rows + side * short, short), short)]
+
+    def far_copy(turn, way):
+        at = turn * 2 + way
+        return remote(
+            piece(turn, z_peer(2), way),
+            relayed.at[turn, way],
+            far_send.at[at],
+            far_recv.at[at],
+            chip(way),
+        )
+
+    def sum_copy(turn, way):
+        at = turn * 2 + way
+        return remote(
+            piece(turn, near(way), 1 - way),
+            sums.at[turn, way, pl.ds((1 - way) * short, short)],
+            sum_send.at[at],
+            sum_recv.at[at],
+            chip(way),
+        )
+
+    def join_copy(turn, way):
+        at = turn * 2 + way
+        return remote(
+            joined.at[turn, way],
+            sums.at[turn, way, pl.ds(way * short, short)],
+            join_send.at[at],
+            join_recv.at[at],
+            chip(way),
+        )
+
+    def hid_copy(turn, way, slot):
+        at = turn * 2 + way
+        return remote(
+            hidden.at[turn, core, slot],
+            hidden.at[turn, core, slot],
+            hid_send.at[at],
+            hid_recv.at[at],
+            chip(way),
+        )
+
+    def lap_copy(turn, way, slot):
+        at = turn * 2 + way
+        there = hidden.at[turn, core, slot, pl.ds(way * short, short)]
+        return remote(there, there, lap_send.at[at], lap_recv.at[at], chip(way))
 
     def hid_pass(turn, at):
         return remote(
@@ -228,33 +234,48 @@
             sibling,
         )
 
-    def out_copy(who, slot):
-        return remote(
-            delta.at[pl.ds(pl.multiple_of(who * rows, rows), rows)],
+    def out_copy(slot, who):
+        return remote(
+            delta.at[pl.ds(pl.multiple_of(slot * rows, rows), rows)],
             deltas.at[slot],
-            out_send.at[who],
+            out_send.at[slot],
             out_recv.at[slot],
             (who, m),
         )
 
+    def out_in(slot):
+        return remote(
+            delta.at[pl.ds(0, rows)], deltas.at[slot], out_send.at[slot], out_recv.at[slot], sibling
+        )
+
     def front(turn):
-        g = group_of(turn)
-
         @pl.loop(0, 4)
         def _(k):
-            who = g * 4 + lax.rem(y + 4 - k, 4)
-
-            @pl.when(who != c)
+            slot = turn * 4 + k
+
+            @pl.when(slot > 0)
             def _():
-                x_copy(who, (who, m)).wait_recv()
-                x_pass(who).start()
+                x_in(slot).wait_recv()
+                x_pass(slot).start()
+
+        for t in range(3):
+
+            @pl.when(turn == t)
+            def _():
+                for k in range(4 * t + 4, 4 * t + 8):
+                    x_copy(k).start()
+
+        @pl.when(turn == 0)
+        def _():
+            for load in loads:
+                load.wait()
+            gain_swap.wait()
 
         @pl.loop(0, 4)
         def _(k):
-            who = g * 4 + lax.rem(y + 4 - k, 4)
-            x_pass(who).wait_recv()
-
-        place = pl.ds(pl.multiple_of(g * group, group), group)
+            x_pass(turn * 4 + k).wait_recv()
+
+        place = pl.ds(pl.multiple_of(turn * group, group), group)
         mixed = own_x[place, :].astype(jnp.float32) * inv_gain_ref[0:1, :]
         square = jnp.sum(mixed * mixed, axis=1, keepdims=True)
         mixed = sib_x[place, :].astype(jnp.float32) * sib_gain[0:1, :]
@@ -278,31 +299,49 @@
             )
             part[turn, :, cols] = total.astype(jnp.bfloat16)
 
-        for k in (2, 1, 3):
-            sum_out(turn, k).start()
+        for way in range(2):
+            far_copy(turn, way).start()
+        for way in range(2):
+            sum_copy(turn, way).start()
+
+    def relay(turn):
+        for way in range(2):
+            far_copy(turn, way).wait_recv()
+            joined[turn, way] = (
+                piece(turn, near(way), way)[...].astype(jnp.float32)
+                + relayed[turn, way].astype(jnp.float32)
+            ).astype(jnp.bfloat16)
+            join_copy(turn, way).start()
 
     def middle(turn):
         total = part[turn, pl.ds(pl.multiple_of(z * rows, rows), rows), :].astype(jnp.float32)
-        for k in range(1, 4):
-            sum_in(turn, k).wait_recv()
-            total += sums[turn, z_peer(k)].astype(jnp.float32)
+        for way in range(2):
+            sum_copy(turn, way).wait_recv()
+            join_copy(turn, way).wait_recv()
+            total += sums[turn, way].astype(jnp.float32)
         square = total[:, both : both + 1] + total[:, both + 64 : both + 65]
         scale = lax.rsqrt(square * (1.0 / (8 * feats)) + EPS)
         gate = total[:, :half] * scale
         up = total[:, half:both] * scale
         hidden[turn, core, z] = (gate / (1.0 + jnp.exp(-gate)) * up).astype(jnp.bfloat16)
-        for k in (2, 1, 3):
-            hid_out(turn, k).start()
+        for way in range(2):
+            hid_copy(turn, way, z).start()
         hid_pass(turn, z).start()
 
+    def lap(turn):
+        for way in range(2):
+            slot = near(1 - way)
+            hid_copy(turn, way, slot).wait_recv()
+            lap_copy(turn, way, slot).start()
+            hid_pass(turn, slot).start()
+
     def back(turn):
-        for k in range(1, 4):
-            hid_in(turn, k).wait_recv()
-            hid_pass(turn, z_peer(k)).start()
+        for way in range(2):
+            lap_copy(turn, way, z_peer(2)).wait_recv()
+        hid_pass(turn, z_peer(2)).start()
         for k in range(4):
             hid_passed(turn, z_peer(k)).wait_recv()
-        g = group_of(turn)
-        place = pl.ds(pl.multiple_of(g * group, group), group)
+        place = pl.ds(pl.multiple_of(turn * group, group), group)
 
         @pl.loop(0, feats // 256)
         def _(tile):
@@ -319,35 +358,34 @@
             )
             delta[place, cols] = total.astype(jnp.bfloat16)
 
-        @pl.loop(0, 4)
-        def _(k):
-            who = g * 4 + lax.rem(y + k, 4)
-
-            @pl.when(who != c)
+        for k in range(4):
+            dx, dy = 0, 0
+            for t in range(4):
+                dx = jnp.where(turn == t, OFFSETS[4 * t + k][0], dx)
+                dy = jnp.where(turn == t, OFFSETS[4 * t + k][1], dy)
+            who = lax.rem(x + dx, 4) * 4 + lax.rem(y + dy, 4)
+            if k > 0:
+                out_copy(turn * 4 + k, who).start()
+            else:
+
+                @pl.when(turn > 0)
+                def _():
+                    out_copy(turn * 4, who).start()
+
+    @pl.loop(0, 8)
+    def _(step):
+        for late, stage in enumerate((front, relay, middle, lap, back)):
+
+            @pl.when((step >= late) & (step < late + 4))
             def _():
-                out_copy(who, c).start()
-
-    @pl.loop(0, 6)
-    def _(step):
-        @pl.when(step < 4)
-        def _():
-            front(step)
-
-        @pl.when((step >= 1) & (step < 5))
-        def _():
-            middle(step - 1)
-
-        @pl.when(step >= 2)
-        def _():
-            back(step - 2)
-
-    total_ref[...] = share_ref[...] + delta[my_rows, :].astype(jnp.float32)
+                stage(step - late)
+
+    total_ref[...] = share_ref[...] + delta[0:rows, :].astype(jnp.float32)
 
     @pl.loop(1, 16)
     def _(k):
-        who = peer(k)
-        out_copy(who, who).wait_recv()
-        total_ref[...] += deltas[who].astype(jnp.float32)
+        out_in(k).wait_recv()
+        total_ref[...] += deltas[k].astype(jnp.float32)
 
     update = (score_ref[:, 0:1] * total_ref[...]).astype(jnp.bfloat16)
     slot_at = lax.broadcasted_iota(jnp.int32, (slots, rows), 0)
@@ -357,22 +395,26 @@
     def box_of(who):
         return pl.ds(pl.multiple_of(who * box, box), box)
 
-    def box_copy(who, slot):
-        return remote(
-            outbox.at[box_of(who)], inbox.at[box_of(slot)], box_send.at[who], box_recv.at[slot], (who, m)
-        )
-
-    @pl.loop(1, 16)
-    def _(k):
-        box_copy(peer(k), c).start()
+    def box_copy(k):
+        who = ahead(c, k)
+        return remote(
+            outbox.at[box_of(who)], inbox.at[box_of(c)], box_send.at[k], box_recv.at[c], (who, m)
+        )
+
+    def box_in(who):
+        return remote(
+            outbox.at[box_of(who)], inbox.at[box_of(who)], box_send.at[0], box_recv.at[who], sibling
+        )
+
+    for k in range(1, 16):
+        box_copy(k).start()
 
     inbox[box_of(c), :] = outbox[box_of(c), :]
     slot_at = lax.broadcasted_iota(jnp.int32, (tokens_ref.shape[0], slots), 1)
     back_to = jnp.where(slot_at == send_ref[:, 0:1], 1.0, 0.0).astype(jnp.bfloat16)
 
-    @pl.loop(1, 16)
-    def _(k):
-        box_copy(peer(k), peer(k)).wait_recv()
+    for k in range(1, 16):
+        box_in(ahead(c, k)).wait_recv()
 
     @pl.loop(0, feats // 256)
     def _(tile):
@@ -380,11 +422,10 @@
         arrived = jnp.dot(back_to, inbox[:, cols], preferred_element_type=jnp.float32)
         out_ref[:, cols] = (tokens_ref[:, cols].astype(jnp.float32) + arrived).astype(jnp.bfloat16)
 
-    @pl.loop(1, 16)
-    def _(k):
-        x_out(k).wait_send()
-        out_copy(peer(k), c).wait_send()
-        box_copy(peer(k), c).wait_send()
+    for k in range(1, 16):
+        x_copy(k).wait_send()
+        out_in(k).wait_send()
+        box_copy(k).wait_send()
 
     @pl.loop(0, 16)
     def _(who):
@@ -392,14 +433,17 @@
 
     @pl.loop(0, 4)
     def _(turn):
-        for k in range(1, 4):
-            sum_out(turn, k).wait_send()
-            hid_out(turn, k).wait_send()
+        for way in range(2):
+            far_copy(turn, way).wait_send()
+            sum_copy(turn, way).wait_send()
+            join_copy(turn, way).wait_send()
+            hid_copy(turn, way, z).wait_send()
+            lap_copy(turn, way, near(1 - way)).wait_send()
         for k in range(4):
             hid_pass(turn, z_peer(k)).wait_send()
 
 
-def feed_forward(scaled, share, score, take, send, tokens, inv_gain, gate_weight, up_weight, down_weight):
+def feed_forward(scaled, share, score, take, send, tokens, inv_gain, gate_weight, up_weight, gate_half, up_half, down_weight):
     rows, feats = scaled.shape
     cols = gate_weight.shape[1]
     half = cols // 2
@@ -409,7 +453,7 @@
     return pl.pallas_call(
         mlp_kernel,
         out_shape=jax.ShapeDtypeStruct(tokens.shape, bf16),
-        in_specs=[vmem] * 7 + [anywhere, anywhere, anywhere],
+        in_specs=[vmem] * 7 + [anywhere] * 5,
         out_specs=vmem,
         scratch_shapes=[
             pltpu.VMEM((16 * rows, feats), bf16),
@@ -418,23 +462,25 @@
             pltpu.VMEM((2 * feats, cols), bf16),
             pltpu.VMEM((cols, feats), bf16),
             pltpu.VMEM((4, 4 * rows, cols + 128), bf16),
-            pltpu.VMEM((4, 4, rows, cols + 128), bf16),
+            pltpu.VMEM((4, 2, rows // 2, cols + 128), bf16),
+            pltpu.VMEM((4, 2, rows // 2, cols + 128), bf16),
+            pltpu.VMEM((4, 2, rows, cols + 128), bf16),
             pltpu.VMEM((4, 2, 4, rows, half), bf16),
             pltpu.VMEM((16 * rows, feats), bf16),
             pltpu.VMEM((16, rows, feats), bf16),
             pltpu.VMEM((rows, feats), jnp.float32),
             pltpu.VMEM((16 * BOX, feats), bf16),
             pltpu.VMEM((16 * BOX, feats), bf16),
-            dma((3,)),
-            dma((3,)),
-            dma((3,)),
+            dma((5,)),
+            dma((1,)),
+            dma((1,)),
         ]
-        + [dma((16,))] * 14,
+        + [dma((16,))] * 20,
         compiler_params=pltpu.CompilerParams(
             collective_id=3, has_side_effects=True, vmem_limit_bytes=56 * 2**20
         ),
         name="feed_forward",
-    )(scaled, share, score, take, send, tokens, inv_gain, gate_weight, up_weight, down_weight)
+    )(scaled, share, score, take, send, tokens, inv_gain, gate_weight, up_weight, gate_half, up_half, down_weight)
 
 
 def attend_kernel(
@@ -447,12 +493,16 @@
     key_ref,
     value_ref,
     out_weight_ref,
+    gate_ref,
+    up_ref,
     cosine_ref,
     sine_ref,
     mlp_gain_ref,
     share_ref,
     scaled_ref,
     score_ref,
+    gate_half_ref,
+    up_half_ref,
     outbox,
     inbox,
     full,
@@ -467,6 +517,8 @@
     delta,
     deltas,
     load_sem,
+    swap_send,
+    swap_recv,
     box_send,
     box_recv,
     row_send,
@@ -497,15 +549,6 @@
     z, core = m // 2, m % 2
     sibling = (c, z * 2 + 1 - core)
 
-    def peer(step):
-        turn = step // 4
-        shift = turn + (turn // 2) * (1 - 2 * (turn % 2))
-        return lax.rem(x + 4 - shift, 4) * 4 + lax.rem(y + step % 4, 4)
-
-    def group_of(turn):
-        shift = turn + (turn // 2) * (1 - 2 * (turn % 2))
-        return lax.rem(x + shift, 4)
-
     def rows_of(who, count=1):
         return pl.ds(pl.multiple_of(who * (rows * count), rows), rows * count)
 
@@ -514,16 +557,14 @@
 
     @pl.loop(0, 16)
     def _(k):
-        @pl.when(k > 0)
-        def _():
-            pl.semaphore_signal(barrier, inc=1, device_id=(peer(k), m), device_id_type=MESH)
-
         @pl.when(jnp.logical_not(is_home & (k // 8 == c % 2) & (k % 8 == m)))
         def _():
             pl.semaphore_signal(
                 barrier, inc=1, device_id=(2 * m + k // 8, k % 8), device_id_type=MESH
             )
 
+    for k in range(1, 16):
+        pl.semaphore_signal(barrier, inc=1, device_id=(ahead(c, k), m), device_id_type=MESH)
     for k in range(1, 4):
         pl.semaphore_signal(
             barrier,
@@ -560,18 +601,21 @@
     inbox[box_of(c), :] = outbox[box_of(c), :]
     pl.semaphore_wait(barrier, jnp.where(is_home, 34, 35))
 
-    def box_copy(who, slot):
-        return remote(
-            outbox.at[box_of(who)], inbox.at[box_of(slot)], box_send.at[who], box_recv.at[slot], (who, m)
-        )
-
-    @pl.loop(1, 16)
-    def _(k):
-        box_copy(peer(k), c).start()
-
-    @pl.loop(1, 16)
-    def _(k):
-        box_copy(peer(k), peer(k)).wait_recv()
+    def box_copy(k):
+        who = ahead(c, k)
+        return remote(
+            outbox.at[box_of(who)], inbox.at[box_of(c)], box_send.at[k], box_recv.at[c], (who, m)
+        )
+
+    def box_in(who):
+        return remote(
+            outbox.at[box_of(who)], inbox.at[box_of(who)], box_send.at[0], box_recv.at[who], sibling
+        )
+
+    for k in range(1, 16):
+        box_copy(k).start()
+    for k in range(1, 16):
+        box_in(ahead(c, k)).wait_recv()
 
     slot_at = lax.broadcasted_iota(jnp.int32, (rows, slots), 1)
     take = jnp.where(slot_at == take_ref[:, 0:1], 1.0, 0.0).astype(jnp.bfloat16)
@@ -617,58 +661,56 @@
         normed[2 * at] = wide[:, :width]
         normed[2 * at + 1] = wide[:, width:]
 
-    def norm_copy(who, slot):
-        return remote(
-            normed.at[who], blocks.at[rows_of(slot)], norm_send.at[who], norm_recv.at[slot], (who, m)
-        )
-
-    @pl.loop(1, 16)
-    def _(k):
-        norm_copy(peer(k), c).start()
-
-    blocks[rows_of(c), :] = normed[c]
+    def norm_copy(k):
+        who = behind(c, k)
+        return remote(
+            normed.at[who], blocks.at[rows_of(k)], norm_send.at[k], norm_recv.at[k], (who, m)
+        )
+
+    def norm_in(slot):
+        return remote(
+            normed.at[0], blocks.at[rows_of(slot)], norm_send.at[slot], norm_recv.at[slot], sibling
+        )
+
+    for k in range(1, 16):
+        norm_copy(k).start()
+    blocks[0:rows, :] = normed[c]
+    half = gate_half_ref.shape[1]
+    others = pl.ds(pl.multiple_of((1 - core) * half, 128), half)
+    swaps = [
+        remote(gate_ref.at[:, others], gate_half_ref, swap_send.at[0], swap_recv.at[0], sibling),
+        remote(up_ref.at[:, others], up_half_ref, swap_send.at[1], swap_recv.at[1], sibling),
+    ]
+    for swap in swaps:
+        swap.start()
     for load in loads:
         load.wait()
 
-    def part_copy(who, slot):
-        return remote(
-            part.at[rows_of(who)], parts.at[slot], part_send.at[who], part_recv.at[slot], (who, m)
-        )
-
-    @pl.loop(0, 4)
-    def _(turn):
-        g = group_of(turn)
-
-        @pl.loop(0, 4)
-        def _(k):
-            who = g * 4 + k
-
-            @pl.when(who != c)
-            def _():
-                norm_copy(who, who).wait_recv()
-
-        here = rows_of(g, 4)
+    def part_copy(k):
+        return remote(
+            part.at[rows_of(k)], parts.at[k], part_send.at[k], part_recv.at[k], (ahead(c, k), m)
+        )
+
+    for turn in range(4):
+        for k in range(max(4 * turn, 1), 4 * turn + 4):
+            norm_in(k).wait_recv()
+        here = rows_of(turn, 4)
         part[here, :] = jnp.dot(
             blocks[here, :], weight[...], preferred_element_type=jnp.float32
         ).astype(jnp.bfloat16)
-
-        @pl.loop(0, 4)
-        def _(k):
-            who = g * 4 + lax.rem(y + k, 4)
-
-            @pl.when(who != c)
-            def _():
-                part_copy(who, c).start()
+        for k in range(max(4 * turn, 1), 4 * turn + 4):
+            part_copy(k).start()
 
     for at in range(0, weight.shape[1], HEAD_DIM):
-        total_at = part[rows_of(c), at : at + HEAD_DIM]
+        total_at = part[0:rows, at : at + HEAD_DIM]
         share_ref[:, at : at + HEAD_DIM] = total_at.astype(jnp.float32)
 
     @pl.loop(1, 16)
     def _(k):
-        who = peer(k)
-        part_copy(who, who).wait_recv()
-        share_ref[:, 0 : weight.shape[1]] += parts[who].astype(jnp.float32)
+        remote(
+            part.at[0:rows], parts.at[k], part_send.at[k], part_recv.at[k], sibling
+        ).wait_recv()
+        share_ref[:, 0 : weight.shape[1]] += parts[k].astype(jnp.float32)
 
     def turned(at):
         head = share_ref[:, at : at + HEAD_DIM]
@@ -680,24 +722,22 @@
     at = q_cols + kv_cols
     key_value[mine, HEAD_DIM : 2 * HEAD_DIM] = share_ref[:, at : at + HEAD_DIM].astype(jnp.bfloat16)
 
-    def kv_copy(k, who):
+    def kv_copy(k, who, device):
         return remote(
             key_value.at[rows_of(who)],
             key_value.at[rows_of(who)],
             kv_send.at[k],
             kv_recv.at[who],
-            (peer(k), m),
-        )
-
-    @pl.loop(1, 16)
-    def _(k):
-        kv_copy(k, c).start()
+            device,
+        )
+
+    for k in range(1, 16):
+        kv_copy(k, c, (behind(c, k), m)).start()
 
     queries = jnp.concatenate([turned(h * HEAD_DIM) for h in range(heads)], axis=0)
 
-    @pl.loop(1, 16)
-    def _(k):
-        kv_copy(k, peer(k)).wait_recv()
+    for k in range(1, 16):
+        kv_copy(k, ahead(c, k), sibling).wait_recv()
 
     keys = 16 * rows
     scores = lax.dot_general(
@@ -722,28 +762,27 @@
         / total
     ).astype(jnp.bfloat16)
     for h in range(heads):
-        attended[mine, h * HEAD_DIM : (h + 1) * HEAD_DIM] = mixed[h * rows : (h + 1) * rows]
-
-    def att_copy(k, who):
-        return remote(
-            attended.at[rows_of(who)],
-            attended.at[rows_of(who)],
+        attended[0:rows, h * HEAD_DIM : (h + 1) * HEAD_DIM] = mixed[h * rows : (h + 1) * rows]
+
+    def att_copy(k):
+        return remote(
+            attended.at[0:rows],
+            attended.at[rows_of(k)],
             att_send.at[k],
-            att_recv.at[who],
-            (peer(k), m),
-        )
-
-    @pl.loop(1, 16)
-    def _(k):
-        att_copy(k, c).start()
+            att_recv.at[k],
+            (behind(c, k), m),
+        )
+
+    for k in range(1, 16):
+        att_copy(k).start()
 
     my_slot = (c % 2) * 8 + m
 
-    def out_copy(who):
-        return remote(
-            delta.at[rows_of(who)],
+    def out_copy(k, who):
+        return remote(
+            delta.at[rows_of(k)],
             deltas.at[my_slot],
-            out_send.at[who],
+            out_send.at[k],
             out_recv.at[my_slot],
             (who, home),
         )
@@ -757,35 +796,25 @@
             (2 * m + slot // 8, slot % 8),
         )
 
-    @pl.loop(0, 4)
-    def _(turn):
-        g = group_of(turn)
-
-        @pl.loop(0, 4)
-        def _(k):
-            who = g * 4 + lax.rem(y + 4 - k, 4)
-
-            @pl.when(who != c)
-            def _():
-                step = turn * 4 + k
-                att_copy(step, who).wait_recv()
-
-        here = rows_of(g, 4)
+    for turn in range(4):
+        for k in range(max(4 * turn, 1), 4 * turn + 4):
+            att_copy(k).wait_recv()
+        here = rows_of(turn, 4)
         delta[here, :] = jnp.dot(
             attended[here, :], out_weight[...], preferred_element_type=jnp.float32
         ).astype(jnp.bfloat16)
-
-        @pl.loop(0, 4)
-        def _(k):
-            who = g * 4 + lax.rem(y + k, 4)
-
-            @pl.when(jnp.logical_not(is_home & (who == c)))
-            def _():
-                out_copy(who).start()
+        for k in range(4 * turn, 4 * turn + 4):
+            if k > 0:
+                out_copy(k, ahead(c, k)).start()
+            else:
+
+                @pl.when(jnp.logical_not(is_home))
+                def _():
+                    out_copy(0, c).start()
 
     @pl.when(is_home)
     def _():
-        deltas[my_slot] = delta[mine, :]
+        deltas[my_slot] = delta[0:rows, :]
 
     share_ref[...] = jnp.zeros_like(share_ref)
 
@@ -809,25 +838,25 @@
     for k in range(4):
         hop(z_block(k)).wait_send()
 
-    @pl.loop(0, 16)
-    def _(k):
-        @pl.when(jnp.logical_not(is_home & (k == c)))
-        def _():
-            out_copy(k).wait_send()
-
-        @pl.when(k != c)
-        def _():
-            box_copy(k, c).wait_send()
-            norm_copy(k, c).wait_send()
-            part_copy(k, c).wait_send()
-
-        @pl.when(k > 0)
-        def _():
-            kv_copy(k, c).wait_send()
-            att_copy(k, c).wait_send()
-
-
-def attend(tokens, send, take, gain, router, query, key, value, out_weight, cosine, sine, mlp_gain):
+    for swap in swaps:
+        swap.wait()
+
+    @pl.when(jnp.logical_not(is_home))
+    def _():
+        out_copy(0, c).wait_send()
+
+    for k in range(1, 16):
+        out_copy(k, ahead(c, k)).wait_send()
+        box_copy(k).wait_send()
+        norm_copy(k).wait_send()
+        part_copy(k).wait_send()
+        kv_copy(k, c, sibling).wait_send()
+        att_copy(k).wait_send()
+
+
+def attend(
+    tokens, send, take, gain, router, query, key, value, out_weight, gate, up, cosine, sine, mlp_gain
+):
     count, slots = take.shape[0], 16 * BOX
     feats = tokens.shape[1]
     width = query.shape[0]
@@ -842,9 +871,11 @@
             jax.ShapeDtypeStruct((count, feats), jnp.float32),
             jax.ShapeDtypeStruct((count, feats), bf16),
             jax.ShapeDtypeStruct((count, 128), jnp.float32),
+            jax.ShapeDtypeStruct((gate.shape[0], gate.shape[1] // 2), bf16),
+            jax.ShapeDtypeStruct((up.shape[0], up.shape[1] // 2), bf16),
         ),
-        in_specs=[vmem] * 5 + [anywhere] * 4 + [vmem] * 3,
-        out_specs=(vmem, vmem, vmem),
+        in_specs=[vmem] * 5 + [anywhere] * 6 + [vmem] * 3,
+        out_specs=(vmem, vmem, vmem, anywhere, anywhere),
         scratch_shapes=[
             pltpu.VMEM((slots, feats), bf16),
             pltpu.VMEM((slots, feats), bf16),
@@ -860,13 +891,15 @@
             pltpu.VMEM((16 * count, out_cols), bf16),
             pltpu.VMEM((16, count, out_cols), bf16),
             dma((4,)),
+            dma((2,)),
+            dma((2,)),
         ]
         + [dma((16,))] * 16,
         compiler_params=pltpu.CompilerParams(
             collective_id=2, has_side_effects=True, vmem_limit_bytes=48 * 2**20
         ),
         name="attend",
-    )(tokens, send, take, gain, router, query, key, value, out_weight, cosine, sine, mlp_gain)
+    )(tokens, send, take, gain, router, query, key, value, out_weight, gate, up, cosine, sine, mlp_gain)
 
 
 def body(
@@ -918,7 +951,7 @@
     angles = kept_pos.astype(jnp.float32)[:, None] * (500000.0 ** (-exponent))[None, :]
     cosine, sine = jnp.cos(angles), jnp.sin(angles)
     later_gain = mlp_gain.astype(jnp.float32)
-    head_share, scaled, score = attend(
+    head_share, scaled, score, gate_half, up_half = attend(
         tokens,
         jnp.broadcast_to(send_index, (8, tok_dev)),
         jnp.broadcast_to(recv_index[:, None], (kept_dev, 128)),
@@ -928,6 +961,8 @@
         key_weight,
         value_weight,
         out_weight,
+        gate_weight,
+        up_weight,
         jnp.concatenate([cosine, cosine], axis=1),
         jnp.concatenate([-sine, sine], axis=1),
         jnp.broadcast_to(later_gain, (8, feature_cols)),
@@ -942,6 +977,8 @@
         jnp.broadcast_to(1.0 / later_gain, (8, feature_cols)),
         gate_weight,
         up_weight,
+        gate_half,
+        up_half,
         down_weight,
     )
 

time: 263 us -> 245 us (0.932)
  the two profiles are of different devices: /device:TPU:6 before, /device:TPU:32 now
where the time goes in v3:
time: 245 us; the launch traced here: 242 us
  Pallas kernels  222 us (91%)
  local copies, waits for them, and re-layouts  14.8 us (6%)
  other arithmetic  4.7 us (2%)
    pallas_call x1, Pallas kernels, feed_forward(): pl.pallas_call(mlp_kernel, out_shape=jax.ShapeDtypeStruct(tokens.shape, b...  124 us
    pallas_call x1, Pallas kernels, attend(): pl.pallas_call(attend_kernel, out_shape=(jax.ShapeDtypeStruct((count, fea...  98 us
    unnamed x19, local copies, waits for them, and re-layouts  10.6 us

profile of v3, /device:TPU:32, one launch (start us, length us, event | category | flops | bytes accessed | tf_op | source)
XLA Modules:
  0.0 241.8 jit_solution(5671049617325513219)
XLA Ops:
  0.0 0.7 fusion.2
  0.8 0.1 select_reduce_fusion.2
  0.9 0.1 select_reduce_fusion.1
  1.0 1.3 add_select_fusion.1
  2.3 0.7 and_select_fusion.1
  3.0 0.1 select_reduce_fusion
  3.0 0.7 subtract_select_fusion
  3.7 0.6 broadcast_in_dim.87.take_ref
  4.3 0.7 broadcast_divide_fusion
  5.0 0.6 broadcast_in_dim.89.inv_gain_ref
  5.6 0.1 broadcast_in_dim.85.take_ref
  5.7 0.7 reshape.47.gain_ref
  6.4 0.7 reshape.49.router_ref
  7.2 0.7 broadcast_in_dim.86.mlp_gain_ref
  7.9 0.2 fusion
  8.1 0.1 pad_maximum_fusion
  8.2 0.8 broadcast_in_dim.88.send_ref
  9.0 0.0 copy-start
  9.0 1.2 copy-done
  10.2 0.0 copy-start.2
  10.2 1.0 copy-done.2
  11.3 1.0 copy-done.3
  12.3 0.9 copy-done.5
  13.2 0.9 copy-done.6
  14.1 98.0 %attend.1 = (f32[64,1024]{1,0:T(8,128)S(1)}, bf16[64,1024]{1,0:T(8,128)(2,1)S(1)}, f32[64,128]{1,0:T(8,128)S(1)}, bf16[1024,896]{1,0:T(8,128)(2,1)S(1)}, bf16[1024,896]{1,0:T(8,128)(2,1)}) custom-call(bf16[512,1024]{1,0:T(8,128)(2,1)S(1)} %copy-done, s32[8,512]{1,0:T(8,128)S(1)} %broadcast_in_dim.80.send_ref, s32[64,128]{1,0:T(8,128)S(1)} %broadcast_in_dim.85.take_ref, ...), custom_call_target="tpu_custom_call" | custom-call | tf_op jit(solution)/shard_map/attend/pallas_call | solution.py:868
  112.2 0.0 copy-start.1
  112.2 1.2 copy-done.1
  113.4 0.7 copy-done.4
  114.1 0.7 copy-done.7
  114.8 0.6 copy-done.8
  115.4 124.1 %feed_forward.1 = bf16[512,1024]{1,0:T(8,128)(2,1)} custom-call(bf16[64,1024]{1,0:T(8,128)(2,1)} %copy-done.7, f32[64,1024]{1,0:T(8,128)} %copy-done.4, f32[64,128]{1,0:T(8,128)} %copy-done.8, s32[8,64]{1,0:T(8,128)} %broadcast_in_dim.87.take_ref, s32[512,128]{1,0:T(8,128)} %broadcast_in_dim.88.send_ref, bf16[512,1024]{1,0:T(8,128)(2,1)} %tokens_ref.3, ...), custom_call_target="tpu_custom_call" | custom-call | tf_op jit(solution)/shard_map/feed_forward/pallas_call | solution.py:453
  239.5 2.3 copy.15
  (9 shorter events, 0.0 us)
Async XLA Ops:
  9.0 1.2 copy-start
  10.2 1.0 copy-start.2
  11.3 1.0 copy-start.3
  12.3 0.9 copy-start.5
  13.2 0.9 copy-start.6
  112.2 1.2 copy-start.1
  113.4 0.7 copy-start.4
  114.1 0.7 copy-start.7
  114.7 0.6 copy-start.8

commit v4 on v3

--- a/solution.py
+++ b/solution.py
@@ -527,6 +527,8 @@
     hop_recv,
     norm_send,
     norm_recv,
+    wide_send,
+    wide_recv,
     part_send,
     part_recv,
     kv_send,
@@ -537,31 +539,35 @@
     out_recv,
 ):
     rows, feats = share_ref.shape
-    width = blocks.shape[1]
+    width = query_ref.shape[0]
     slots = outbox.shape[0]
     box = slots // 16
     group = 4 * rows
+    cols = weight.shape[1]
     q_cols, kv_cols = query_ref.shape[1], key_ref.shape[1]
     heads = q_cols // HEAD_DIM
     c, m = lax.axis_index("ctx"), lax.axis_index("mp")
     x, y = c // 4, c % 4
-    home = c // 2
     z, core = m // 2, m % 2
     sibling = (c, z * 2 + 1 - core)
 
     def rows_of(who, count=1):
         return pl.ds(pl.multiple_of(who * (rows * count), rows), rows * count)
 
-    is_home = m == home
+    is_home = x == z
     barrier = pltpu.get_barrier_semaphore()
 
-    @pl.loop(0, 16)
+    def x_peer(k):
+        return (lax.rem(x + k, 4) * 4 + y, m)
+
+    def y_peer(k):
+        return (x * 4 + lax.rem(y + k, 4), m)
+
+    @pl.loop(0, 8)
     def _(k):
-        @pl.when(jnp.logical_not(is_home & (k // 8 == c % 2) & (k % 8 == m)))
+        @pl.when(jnp.logical_not(is_home & (k == m)))
         def _():
-            pl.semaphore_signal(
-                barrier, inc=1, device_id=(2 * m + k // 8, k % 8), device_id_type=MESH
-            )
+            pl.semaphore_signal(barrier, inc=1, device_id=(z * 4 + y, k), device_id_type=MESH)
 
     for k in range(1, 16):
         pl.semaphore_signal(barrier, inc=1, device_id=(ahead(c, k), m), device_id_type=MESH)
@@ -574,13 +580,14 @@
         )
     pl.semaphore_signal(barrier, inc=1, device_id=sibling, device_id_type=MESH)
 
+    band = pl.ds(pl.multiple_of(y * width, width), width)
     loads = [
-        pltpu.make_async_copy(query_ref, weight.at[:, pl.ds(0, q_cols)], load_sem.at[0]),
-        pltpu.make_async_copy(key_ref, weight.at[:, pl.ds(q_cols, kv_cols)], load_sem.at[1]),
+        pltpu.make_async_copy(query_ref, weight.at[band, pl.ds(0, q_cols)], load_sem.at[0]),
+        pltpu.make_async_copy(key_ref, weight.at[band, pl.ds(q_cols, kv_cols)], load_sem.at[1]),
         pltpu.make_async_copy(
-            value_ref, weight.at[:, pl.ds(q_cols + kv_cols, kv_cols)], load_sem.at[2]
+            value_ref, weight.at[band, pl.ds(q_cols + kv_cols, kv_cols)], load_sem.at[2]
         ),
-        pltpu.make_async_copy(out_weight_ref, out_weight, load_sem.at[3]),
+        pltpu.make_async_copy(out_weight_ref, out_weight.at[y], load_sem.at[3]),
     ]
     for load in loads:
         load.start()
@@ -599,7 +606,7 @@
         return pl.ds(pl.multiple_of(who * box, box), box)
 
     inbox[box_of(c), :] = outbox[box_of(c), :]
-    pl.semaphore_wait(barrier, jnp.where(is_home, 34, 35))
+    pl.semaphore_wait(barrier, jnp.where(is_home, 26, 27))
 
     def box_copy(k):
         who = ahead(c, k)
@@ -612,8 +619,37 @@
             outbox.at[box_of(who)], inbox.at[box_of(who)], box_send.at[0], box_recv.at[who], sibling
         )
 
+    def weight_copy(k):
+        return remote(
+            weight.at[band], weight.at[band], wide_send.at[k], wide_recv.at[k], y_peer(k)
+        )
+
+    def out_weight_copy(k):
+        return remote(
+            out_weight.at[y],
+            out_weight.at[y],
+            wide_send.at[4 + k],
+            wide_recv.at[4 + k],
+            y_peer(k),
+        )
+
+    def weight_lap(k):
+        whose = lax.rem(y + 4 - k, 4)
+        start = whose * width + (k // 2) * (width // 2)
+        there = weight.at[pl.ds(pl.multiple_of(start, width // 2), width // 2)]
+        return remote(there, there, wide_send.at[k - 1], wide_recv.at[k - 1], y_peer(k))
+
+    def out_weight_lap(k):
+        whose = lax.rem(y + 4 - k, 4)
+        there = out_weight.at[whose, pl.ds((k // 2) * (width // 2), width // 2)]
+        return remote(there, there, wide_send.at[k + 3], wide_recv.at[k + 3], y_peer(k))
+
     for k in range(1, 16):
         box_copy(k).start()
+    for load in loads:
+        load.wait()
+    for k in (1, 3):
+        weight_copy(k).start()
     for k in range(1, 16):
         box_in(ahead(c, k)).wait_recv()
 
@@ -648,6 +684,9 @@
     for k in (0, 1, 3, 2):
         hop(z_sibling(k)).wait_recv()
 
+    for k in (1, 3):
+        weight_copy(k).wait_recv()
+        weight_lap(k).start()
     square, route = 0.0, 0.0
     for at in range(8):
         wide = full[at].astype(jnp.float32)
@@ -658,23 +697,22 @@
     for at in range(8):
         wide = full[at].astype(jnp.float32) * scale * gain_ref[at : at + 1, :]
         wide = wide.astype(jnp.bfloat16)
-        normed[2 * at] = wide[:, :width]
-        normed[2 * at + 1] = wide[:, width:]
+        normed[at] = wide
 
     def norm_copy(k):
-        who = behind(c, k)
-        return remote(
-            normed.at[who], blocks.at[rows_of(k)], norm_send.at[k], norm_recv.at[k], (who, m)
-        )
-
-    def norm_in(slot):
-        return remote(
-            normed.at[0], blocks.at[rows_of(slot)], norm_send.at[slot], norm_recv.at[slot], sibling
-        )
-
-    for k in range(1, 16):
+        to = lax.rem(x + 4 - k, 4)
+        return remote(
+            normed.at[pl.ds(2 * to, 2)],
+            blocks.at[:, k],
+            norm_send.at[k],
+            norm_recv.at[k],
+            (to * 4 + y, m),
+        )
+
+    for k in (1, 3, 2):
         norm_copy(k).start()
-    blocks[0:rows, :] = normed[c]
+    blocks[0, 0] = normed[2 * x]
+    blocks[1, 0] = normed[2 * x + 1]
     half = gate_half_ref.shape[1]
     others = pl.ds(pl.multiple_of((1 - core) * half, 128), half)
     swaps = [
@@ -683,34 +721,38 @@
     ]
     for swap in swaps:
         swap.start()
-    for load in loads:
-        load.wait()
 
     def part_copy(k):
-        return remote(
-            part.at[rows_of(k)], parts.at[k], part_send.at[k], part_recv.at[k], (ahead(c, k), m)
-        )
-
-    for turn in range(4):
-        for k in range(max(4 * turn, 1), 4 * turn + 4):
-            norm_in(k).wait_recv()
-        here = rows_of(turn, 4)
-        part[here, :] = jnp.dot(
-            blocks[here, :], weight[...], preferred_element_type=jnp.float32
-        ).astype(jnp.bfloat16)
-        for k in range(max(4 * turn, 1), 4 * turn + 4):
-            part_copy(k).start()
-
-    for at in range(0, weight.shape[1], HEAD_DIM):
-        total_at = part[0:rows, at : at + HEAD_DIM]
-        share_ref[:, at : at + HEAD_DIM] = total_at.astype(jnp.float32)
-
-    @pl.loop(1, 16)
-    def _(k):
-        remote(
-            part.at[0:rows], parts.at[k], part_send.at[k], part_recv.at[k], sibling
-        ).wait_recv()
-        share_ref[:, 0 : weight.shape[1]] += parts[k].astype(jnp.float32)
+        return remote(part.at[rows_of(k)], parts.at[k], part_send.at[k], part_recv.at[k], x_peer(k))
+
+    for k in (1, 3, 2):
+        norm_copy(k).wait_recv()
+    for k in (1, 3):
+        weight_lap(k).wait_recv()
+    for k in (1, 3):
+        out_weight_copy(k).start()
+
+    @pl.loop(0, cols // 256)
+    def _(tile):
+        at = pl.ds(pl.multiple_of(tile * 256, 256), 256)
+        total = jnp.dot(
+            blocks[0].reshape(group, feats),
+            weight[pl.ds(0, feats), at],
+            preferred_element_type=jnp.float32,
+        )
+        total += jnp.dot(
+            blocks[1].reshape(group, feats),
+            weight[pl.ds(feats, feats), at],
+            preferred_element_type=jnp.float32,
+        )
+        part[:, at] = total.astype(jnp.bfloat16)
+        share_ref[:, at] = total[0:rows]
+
+    for k in (1, 3, 2):
+        part_copy(k).start()
+    for k in (1, 3, 2):
+        part_copy(k).wait_recv()
+        share_ref[:, 0:cols] += parts[k].astype(jnp.float32)
 
     def turned(at):
         head = share_ref[:, at : at + HEAD_DIM]
@@ -738,6 +780,9 @@
 
     for k in range(1, 16):
         kv_copy(k, ahead(c, k), sibling).wait_recv()
+    for k in (1, 3):
+        out_weight_copy(k).wait_recv()
+        out_weight_lap(k).start()
 
     keys = 16 * rows
     scores = lax.dot_general(
@@ -765,70 +810,67 @@
         attended[0:rows, h * HEAD_DIM : (h + 1) * HEAD_DIM] = mixed[h * rows : (h + 1) * rows]
 
     def att_copy(k):
+        to = lax.rem(x + 4 - k, 4)
         return remote(
             attended.at[0:rows],
             attended.at[rows_of(k)],
             att_send.at[k],
             att_recv.at[k],
-            (behind(c, k), m),
-        )
-
-    for k in range(1, 16):
+            (to * 4 + y, m),
+        )
+
+    for k in (1, 3, 2):
         att_copy(k).start()
 
-    my_slot = (c % 2) * 8 + m
-
-    def out_copy(k, who):
-        return remote(
-            delta.at[rows_of(k)],
-            deltas.at[my_slot],
-            out_send.at[k],
-            out_recv.at[my_slot],
-            (who, home),
+    def out_copy(k, side):
+        return remote(
+            delta.at[side, rows_of(k)],
+            deltas.at[m],
+            out_send.at[2 * k + side],
+            out_recv.at[m],
+            (lax.rem(x + k, 4) * 4 + y, 2 * x + side),
         )
 
     def out_in(slot):
         return remote(
-            delta.at[pl.ds(0, rows)],
+            delta.at[0, pl.ds(0, rows)],
             deltas.at[slot],
             out_send.at[slot],
             out_recv.at[slot],
-            (2 * m + slot // 8, slot % 8),
-        )
-
-    for turn in range(4):
-        for k in range(max(4 * turn, 1), 4 * turn + 4):
-            att_copy(k).wait_recv()
-        here = rows_of(turn, 4)
-        delta[here, :] = jnp.dot(
-            attended[here, :], out_weight[...], preferred_element_type=jnp.float32
-        ).astype(jnp.bfloat16)
-        for k in range(4 * turn, 4 * turn + 4):
-            if k > 0:
-                out_copy(k, ahead(c, k)).start()
-            else:
-
-                @pl.when(jnp.logical_not(is_home))
-                def _():
-                    out_copy(0, c).start()
+            sibling,
+        )
+
+    for k in (1, 3):
+        out_weight_lap(k).wait_recv()
+    for k in (1, 3, 2):
+        att_copy(k).wait_recv()
+    for side in range(2):
+        for at in range(2):
+            delta[side, :, at * width : (at + 1) * width] = jnp.dot(
+                attended[...], out_weight[2 * side + at], preferred_element_type=jnp.float32
+            ).astype(jnp.bfloat16)
+        for k in (2, 1, 3):
+            out_copy(k, side).start()
+
+        @pl.when(jnp.logical_not(is_home & (side == core)))
+        def _():
+            out_copy(0, side).start()
 
     @pl.when(is_home)
     def _():
-        deltas[my_slot] = delta[0:rows, :]
+        deltas[m] = delta[core, 0:rows, :]
 
     share_ref[...] = jnp.zeros_like(share_ref)
 
-    for side in range(2):
-
-        @pl.loop(0, 8)
-        def _(k):
-            slot = side * 8 + lax.rem(k + m, 8)
-
-            @pl.when(jnp.logical_not(is_home & (slot == my_slot)))
-            def _():
-                out_in(slot).wait_recv()
-
-            share_ref[:, side * width : (side + 1) * width] += deltas[slot].astype(jnp.float32)
+    @pl.loop(0, 8)
+    def _(k):
+        slot = lax.rem(k + m, 8)
+
+        @pl.when(jnp.logical_not(is_home & (slot == m)))
+        def _():
+            out_in(slot).wait_recv()
+
+        share_ref[...] += deltas[slot].astype(jnp.float32)
 
     mixed = full[m].astype(jnp.float32) + share_ref[...]
     scaled_ref[...] = (mixed * mlp_gain_ref[0:1, :]).astype(jnp.bfloat16)
@@ -841,17 +883,26 @@
     for swap in swaps:
         swap.wait()
 
-    @pl.when(jnp.logical_not(is_home))
-    def _():
-        out_copy(0, c).wait_send()
-
-    for k in range(1, 16):
-        out_copy(k, ahead(c, k)).wait_send()
-        box_copy(k).wait_send()
+    for k in (1, 3):
+        weight_copy(k).wait_send()
+        weight_lap(k).wait_send()
+        out_weight_copy(k).wait_send()
+        out_weight_lap(k).wait_send()
+    for side in range(2):
+        for k in range(1, 4):
+            out_copy(k, side).wait_send()
+
+        @pl.when(jnp.logical_not(is_home & (side == core)))
+        def _():
+            out_copy(0, side).wait_send()
+
+    for k in range(1, 4):
         norm_copy(k).wait_send()
         part_copy(k).wait_send()
+        att_copy(k).wait_send()
+    for k in range(1, 16):
+        box_copy(k).wait_send()
         kv_copy(k, c, sibling).wait_send()
-        att_copy(k).wait_send()
 
 
 def attend(
@@ -861,7 +912,6 @@
     feats = tokens.shape[1]
     width = query.shape[0]
     cols = query.shape[1] + key.shape[1] + value.shape[1]
-    out_cols = out_weight.shape[1]
     dma = pltpu.SemaphoreType.DMA
     bf16 = jnp.bfloat16
     vmem, anywhere = pl.BlockSpec(memory_space=pltpu.VMEM), pl.BlockSpec(memory_space=pl.ANY)
@@ -880,21 +930,21 @@
             pltpu.VMEM((slots, feats), bf16),
             pltpu.VMEM((slots, feats), bf16),
             pltpu.VMEM((8, count, feats), bf16),
-            pltpu.VMEM((16, count, width), bf16),
-            pltpu.VMEM((16 * count, width), bf16),
-            pltpu.VMEM((width, cols), bf16),
-            pltpu.VMEM(out_weight.shape, bf16),
-            pltpu.VMEM((16 * count, cols), bf16),
-            pltpu.VMEM((16, count, cols), bf16),
+            pltpu.VMEM((8, count, feats), bf16),
+            pltpu.VMEM((2, 4, count, feats), bf16),
+            pltpu.VMEM((4 * width, cols), bf16),
+            pltpu.VMEM((4, *out_weight.shape), bf16),
+            pltpu.VMEM((4 * count, cols), bf16),
+            pltpu.VMEM((4, count, cols), bf16),
             pltpu.VMEM((16 * count, 2 * HEAD_DIM), bf16),
-            pltpu.VMEM((16 * count, query.shape[1]), bf16),
-            pltpu.VMEM((16 * count, out_cols), bf16),
-            pltpu.VMEM((16, count, out_cols), bf16),
+            pltpu.VMEM((4 * count, query.shape[1]), bf16),
+            pltpu.VMEM((2, 4 * count, feats), bf16),
+            pltpu.VMEM((8, count, feats), bf16),
             dma((4,)),
             dma((2,)),
             dma((2,)),
         ]
-        + [dma((16,))] * 16,
+        + [dma((16,))] * 18,
         compiler_params=pltpu.CompilerParams(
             collective_id=2, has_side_effects=True, vmem_limit_bytes=48 * 2**20
         ),

time: 245 us -> 220 us (0.90); the launches traced: 242 us -> 219 us
  Pallas kernels: 222 us -> 200 us
    pallas_call x1, Pallas kernels: 98 us -> 84.2 us  [attend(): pl.pallas_call(attend_kernel, out_shape=(jax.ShapeDtypeStruct((count, fea...]
    pallas_call x1, Pallas kernels: 124 us -> 116 us  [feed_forward(): pl.pallas_call(mlp_kernel, out_shape=jax.ShapeDtypeStruct(tokens.shape, b...]
where the time goes in v4:
time: 220 us; the launch traced here: 219 us
  Pallas kernels  200 us (91%)
  local copies, waits for them, and re-layouts  14.8 us (7%)
  other arithmetic  4.7 us (2%)
    pallas_call x1, Pallas kernels, feed_forward(): pl.pallas_call(mlp_kernel, out_shape=jax.ShapeDtypeStruct(tokens.shape, b...  116 us
    pallas_call x1, Pallas kernels, attend(): pl.pallas_call(attend_kernel, out_shape=(jax.ShapeDtypeStruct((count, fea...  84.2 us
    unnamed x19, local copies, waits for them, and re-layouts  10.6 us

profile of v4, /device:TPU:32, one launch (start us, length us, event | category | flops | bytes accessed | tf_op | source)
XLA Modules:
  0.0 219.5 jit_solution(14518943642769367554)
XLA Ops:
  0.0 0.7 fusion.2
  0.8 0.1 select_reduce_fusion.2
  0.9 0.1 select_reduce_fusion.1
  1.0 1.3 add_select_fusion.1
  2.3 0.7 and_select_fusion.1
  3.0 0.1 select_reduce_fusion
  3.0 0.7 subtract_select_fusion
  3.7 0.6 broadcast_in_dim.87.take_ref
  4.3 0.7 broadcast_divide_fusion
  5.0 0.6 broadcast_in_dim.89.inv_gain_ref
  5.6 0.1 broadcast_in_dim.85.take_ref
  5.7 0.7 reshape.47.gain_ref
  6.4 0.7 reshape.49.router_ref
  7.2 0.7 broadcast_in_dim.86.mlp_gain_ref
  7.9 0.2 fusion
  8.1 0.1 pad_maximum_fusion
  8.2 0.8 broadcast_in_dim.88.send_ref
  9.0 0.0 copy-start
  9.0 1.2 copy-done
  10.2 0.0 copy-start.2
  10.2 1.0 copy-done.2
  11.3 1.0 copy-done.3
  12.3 0.9 copy-done.5
  13.2 0.9 copy-done.6
  14.1 84.2 %attend.1 = (f32[64,1024]{1,0:T(8,128)S(1)}, bf16[64,1024]{1,0:T(8,128)(2,1)S(1)}, f32[64,128]{1,0:T(8,128)S(1)}, bf16[1024,896]{1,0:T(8,128)(2,1)S(1)}, bf16[1024,896]{1,0:T(8,128)(2,1)}) custom-call(bf16[512,1024]{1,0:T(8,128)(2,1)S(1)} %copy-done, s32[8,512]{1,0:T(8,128)S(1)} %broadcast_in_dim.80.send_ref, s32[64,128]{1,0:T(8,128)S(1)} %broadcast_in_dim.85.take_ref, ...), custom_call_target="tpu_custom_call" | custom-call | tf_op jit(solution)/shard_map/attend/pallas_call | solution.py:918
  98.3 0.0 copy-start.1
  98.3 1.2 copy-done.1
  99.5 0.7 copy-done.4
  100.2 0.7 copy-done.7
  100.9 0.6 copy-done.8
  101.5 115.7 %feed_forward.1 = bf16[512,1024]{1,0:T(8,128)(2,1)} custom-call(bf16[64,1024]{1,0:T(8,128)(2,1)} %copy-done.7, f32[64,1024]{1,0:T(8,128)} %copy-done.4, f32[64,128]{1,0:T(8,128)} %copy-done.8, s32[8,64]{1,0:T(8,128)} %broadcast_in_dim.87.take_ref, s32[512,128]{1,0:T(8,128)} %broadcast_in_dim.88.send_ref, bf16[512,1024]{1,0:T(8,128)(2,1)} %tokens_ref.3, ...), custom_call_target="tpu_custom_call" | custom-call | tf_op jit(solution)/shard_map/feed_forward/pallas_call | solution.py:453
  217.2 2.3 %copy.15 = bf16[512,1024]{1,0:T(8,128)(2,1)} copy(bf16[512,1024]{1,0:T(8,128)(2,1)} %feed_forward.1) | data formatting | bytes 2097152
  (9 shorter events, 0.0 us)
Async XLA Ops:
  9.0 1.2 copy-start
  10.2 1.0 copy-start.2
  11.3 1.0 copy-start.3
  12.3 0.9 copy-start.5
  13.2 0.9 copy-start.6
  98.3 1.2 copy-start.1
  99.5 0.7 copy-start.4
  100.2 0.7 copy-start.7
  100.9 0.6 copy-start.8

commit v5 on v4

--- a/solution.py
+++ b/solution.py
@@ -8,6 +8,7 @@
 
 HEAD_DIM = 128
 BOX = 16
+VMEM_BYTES = 60 * 2**20
 MESH = pl.DeviceIdType.MESH
 OFFSETS = (
     (0, 0), (0, 1), (1, 0), (0, 3), (3, 0), (1, 1), (3, 3), (1, 3),
@@ -24,6 +25,23 @@
 def behind(c, k):
     dx, dy = OFFSETS[k]
     return lax.rem(c // 4 + 4 - dx, 4) * 4 + lax.rem(c % 4 + 4 - dy, 4)
+
+
+def send_slots(destination, kept):
+    owner, slot = destination // kept, destination % kept
+    going = destination >= 0
+    order = jnp.where(going, slot * 16 + owner, 16 * kept)
+    first = (jnp.min(order) - owner + 15) // 16
+    return jnp.where(going, owner * BOX + slot - first, 16 * BOX)
+
+
+def take_slots(row, column, shard, axis):
+    kept = row.shape[1]
+    same = column // shard == row // shard
+    at = lax.broadcasted_iota(jnp.int32, (kept, kept), axis)
+    first = jnp.min(jnp.where(same, at, kept), axis=axis, keepdims=True)
+    mine = row if axis == 0 else column
+    return mine // shard * BOX + lax.broadcasted_iota(jnp.int32, mine.shape, 1 - axis) - first
 
 
 def remote(source, target, sent, landed, device):
@@ -41,10 +59,10 @@
     x_ref,
     share_ref,
     score_ref,
-    take_ref,
-    send_ref,
-    tokens_ref,
-    inv_gain_ref,
+    kept_row_ref,
+    kept_column_ref,
+    destination_ref,
+    gains_ref,
     gate_ref,
     up_ref,
     gate_half_ref,
@@ -53,6 +71,7 @@
     out_ref,
     own_x,
     sib_x,
+    own_gain,
     sib_gain,
     weight,
     down,
@@ -138,6 +157,7 @@
     for load in loads:
         load.start()
     own_x[0:rows, :] = x_ref[...]
+    own_gain[...] = 1.0 / gains_ref[16:24, :]
     pl.semaphore_wait(barrier, 18)
 
     def x_copy(k):
@@ -156,7 +176,7 @@
 
     for k in range(1, 4):
         x_copy(k).start()
-    gain_swap = remote(inv_gain_ref, sib_gain, swap_send.at[0], swap_recv.at[0], sibling)
+    gain_swap = remote(own_gain, sib_gain, swap_send.at[0], swap_recv.at[0], sibling)
     x_pass(0).start()
     gain_swap.start()
 
@@ -276,7 +296,7 @@
             x_pass(turn * 4 + k).wait_recv()
 
         place = pl.ds(pl.multiple_of(turn * group, group), group)
-        mixed = own_x[place, :].astype(jnp.float32) * inv_gain_ref[0:1, :]
+        mixed = own_x[place, :].astype(jnp.float32) * own_gain[0:1, :]
         square = jnp.sum(mixed * mixed, axis=1, keepdims=True)
         mixed = sib_x[place, :].astype(jnp.float32) * sib_gain[0:1, :]
         square = square + jnp.sum(mixed * mixed, axis=1, keepdims=True)
@@ -389,7 +409,9 @@
 
     update = (score_ref[:, 0:1] * total_ref[...]).astype(jnp.bfloat16)
     slot_at = lax.broadcasted_iota(jnp.int32, (slots, rows), 0)
-    give = jnp.where(slot_at == take_ref[0:1, :], 1.0, 0.0).astype(jnp.bfloat16)
+    shard = destination_ref.shape[1]
+    taken = take_slots(kept_row_ref[0:1, :], kept_column_ref[:, 0:1], shard, 0)
+    give = jnp.where(slot_at == taken, 1.0, 0.0).astype(jnp.bfloat16)
     outbox[...] = jnp.dot(give, update, preferred_element_type=jnp.float32).astype(jnp.bfloat16)
 
     def box_of(who):
@@ -410,8 +432,9 @@
         box_copy(k).start()
 
     inbox[box_of(c), :] = outbox[box_of(c), :]
-    slot_at = lax.broadcasted_iota(jnp.int32, (tokens_ref.shape[0], slots), 1)
-    back_to = jnp.where(slot_at == send_ref[:, 0:1], 1.0, 0.0).astype(jnp.bfloat16)
+    slot_at = lax.broadcasted_iota(jnp.int32, (slots, shard), 0)
+    sent = send_slots(destination_ref[0:1, :], rows)
+    back_to = jnp.where(slot_at == sent, 1.0, 0.0).T.astype(jnp.bfloat16)
 
     for k in range(1, 16):
         box_in(ahead(c, k)).wait_recv()
@@ -419,8 +442,9 @@
     @pl.loop(0, feats // 256)
     def _(tile):
         cols = pl.ds(pl.multiple_of(tile * 256, 256), 256)
-        arrived = jnp.dot(back_to, inbox[:, cols], preferred_element_type=jnp.float32)
-        out_ref[:, cols] = (tokens_ref[:, cols].astype(jnp.float32) + arrived).astype(jnp.bfloat16)
+        out_ref[:, cols] = jnp.dot(
+            back_to, inbox[:, cols], preferred_element_type=jnp.float32
+        ).astype(jnp.bfloat16)
 
     for k in range(1, 16):
         x_copy(k).wait_send()
@@ -443,7 +467,20 @@
             hid_pass(turn, z_peer(k)).wait_send()
 
 
-def feed_forward(scaled, share, score, take, send, tokens, inv_gain, gate_weight, up_weight, gate_half, up_half, down_weight):
+def feed_forward(
+    scaled,
+    share,
+    score,
+    kept_row,
+    kept_column,
+    destination,
+    gains,
+    gate_weight,
+    up_weight,
+    gate_half,
+    up_half,
+    down_weight,
+):
     rows, feats = scaled.shape
     cols = gate_weight.shape[1]
     half = cols // 2
@@ -452,12 +489,13 @@
     vmem, anywhere = pl.BlockSpec(memory_space=pltpu.VMEM), pl.BlockSpec(memory_space=pl.ANY)
     return pl.pallas_call(
         mlp_kernel,
-        out_shape=jax.ShapeDtypeStruct(tokens.shape, bf16),
+        out_shape=jax.ShapeDtypeStruct((destination.shape[1], feats), bf16),
         in_specs=[vmem] * 7 + [anywhere] * 5,
         out_specs=vmem,
         scratch_shapes=[
             pltpu.VMEM((16 * rows, feats), bf16),
             pltpu.VMEM((16 * rows, feats), bf16),
+            pltpu.VMEM((8, feats), jnp.float32),
             pltpu.VMEM((8, feats), jnp.float32),
             pltpu.VMEM((2 * feats, cols), bf16),
             pltpu.VMEM((cols, feats), bf16),
@@ -477,18 +515,31 @@
         ]
         + [dma((16,))] * 20,
         compiler_params=pltpu.CompilerParams(
-            collective_id=3, has_side_effects=True, vmem_limit_bytes=56 * 2**20
+            collective_id=3, has_side_effects=True, vmem_limit_bytes=VMEM_BYTES
         ),
         name="feed_forward",
-    )(scaled, share, score, take, send, tokens, inv_gain, gate_weight, up_weight, gate_half, up_half, down_weight)
+    )(
+        scaled,
+        share,
+        score,
+        kept_row,
+        kept_column,
+        destination,
+        gains,
+        gate_weight,
+        up_weight,
+        gate_half,
+        up_half,
+        down_weight,
+    )
 
 
 def attend_kernel(
     tokens_ref,
-    send_ref,
-    take_ref,
-    gain_ref,
-    router_ref,
+    destination_ref,
+    kept_row_ref,
+    kept_column_ref,
+    gains_ref,
     query_ref,
     key_ref,
     value_ref,
@@ -497,7 +548,6 @@
     up_ref,
     cosine_ref,
     sine_ref,
-    mlp_gain_ref,
     share_ref,
     scaled_ref,
     score_ref,
@@ -593,7 +643,8 @@
         load.start()
 
     slot_at = lax.broadcasted_iota(jnp.int32, (slots, tokens_ref.shape[0]), 0)
-    pick = jnp.where(slot_at == send_ref[0:1, :], 1.0, 0.0).astype(jnp.bfloat16)
+    sent = send_slots(destination_ref[0:1, :], rows)
+    pick = jnp.where(slot_at == sent, 1.0, 0.0).astype(jnp.bfloat16)
 
     @pl.loop(0, feats // 256)
     def _(tile):
@@ -654,7 +705,8 @@
         box_in(ahead(c, k)).wait_recv()
 
     slot_at = lax.broadcasted_iota(jnp.int32, (rows, slots), 1)
-    take = jnp.where(slot_at == take_ref[:, 0:1], 1.0, 0.0).astype(jnp.bfloat16)
+    taken = take_slots(kept_row_ref[0:1, :], kept_column_ref[:, 0:1], tokens_ref.shape[0], 1)
+    take = jnp.where(slot_at == taken, 1.0, 0.0).astype(jnp.bfloat16)
     full[m] = jnp.dot(take, inbox[...], preferred_element_type=jnp.float32).astype(jnp.bfloat16)
 
     def row_copy(k, who):
@@ -691,11 +743,11 @@
     for at in range(8):
         wide = full[at].astype(jnp.float32)
         square += jnp.sum(wide * wide, axis=1, keepdims=True)
-        route += jnp.sum(wide * router_ref[at : at + 1, :], axis=1, keepdims=True)
+        route += jnp.sum(wide * gains_ref[8 + at : 9 + at, :], axis=1, keepdims=True)
     scale = lax.rsqrt(square * (1.0 / (8 * feats)) + EPS)
     score_ref[...] = jnp.broadcast_to(1.0 / (1.0 + jnp.exp(-route)), score_ref.shape)
     for at in range(8):
-        wide = full[at].astype(jnp.float32) * scale * gain_ref[at : at + 1, :]
+        wide = full[at].astype(jnp.float32) * scale * gains_ref[at : at + 1, :]
         wide = wide.astype(jnp.bfloat16)
         normed[at] = wide
 
@@ -873,7 +925,7 @@
         share_ref[...] += deltas[slot].astype(jnp.float32)
 
     mixed = full[m].astype(jnp.float32) + share_ref[...]
-    scaled_ref[...] = (mixed * mlp_gain_ref[0:1, :]).astype(jnp.bfloat16)
+    scaled_ref[...] = (mixed * gains_ref[16:17, :]).astype(jnp.bfloat16)
 
     for k in range(1, 4):
         row_copy(k, m).wait_send()
@@ -906,9 +958,9 @@
 
 
 def attend(
-    tokens, send, take, gain, router, query, key, value, out_weight, gate, up, cosine, sine, mlp_gain
+    tokens, destination, kept_row, kept_column, gains, query, key, value, out_weight, gate, up, cosine, sine
 ):
-    count, slots = take.shape[0], 16 * BOX
+    count, slots = kept_column.shape[0], 16 * BOX
     feats = tokens.shape[1]
     width = query.shape[0]
     cols = query.shape[1] + key.shape[1] + value.shape[1]
@@ -924,7 +976,7 @@
             jax.ShapeDtypeStruct((gate.shape[0], gate.shape[1] // 2), bf16),
             jax.ShapeDtypeStruct((up.shape[0], up.shape[1] // 2), bf16),
         ),
-        in_specs=[vmem] * 5 + [anywhere] * 6 + [vmem] * 3,
+        in_specs=[vmem] * 5 + [anywhere] * 6 + [vmem] * 2,
         out_specs=(vmem, vmem, vmem, anywhere, anywhere),
         scratch_shapes=[
             pltpu.VMEM((slots, feats), bf16),
@@ -946,10 +998,24 @@
         ]
         + [dma((16,))] * 18,
         compiler_params=pltpu.CompilerParams(
-            collective_id=2, has_side_effects=True, vmem_limit_bytes=48 * 2**20
+            collective_id=2, has_side_effects=True, vmem_limit_bytes=VMEM_BYTES
         ),
         name="attend",
-    )(tokens, send, take, gain, router, query, key, value, out_weight, gate, up, cosine, sine, mlp_gain)
+    )(
+        tokens,
+        destination,
+        kept_row,
+        kept_column,
+        gains,
+        query,
+        key,
+        value,
+        out_weight,
+        gate,
+        up,
+        cosine,
+        sine,
+    )
 
 
 def body(
@@ -967,46 +1033,28 @@
     destination,
     kept_pos,
 ):
-    ctx_count = lax.axis_size("ctx")
-    tok_dev = tokens.shape[0]
+    tok_dev, feature_cols = tokens.shape
     kept_dev = kept_pos.shape[0]
-    feature_cols = tokens.shape[1]
-    capacity = BOX
-    slots_all = ctx_count * capacity
-    peer_ids = jnp.arange(ctx_count, dtype=jnp.int32)
-    is_kept = destination >= 0
-    owner_ids = destination // kept_dev
-    slot_ids = destination % kept_dev
-    kept_order = slot_ids * ctx_count + owner_ids
-    first_order = jnp.min(jnp.where(is_kept, kept_order, ctx_count * kept_dev))
-    first_slots = (first_order - peer_ids + ctx_count - 1) // ctx_count
-    owner_match = owner_ids[:, None] == peer_ids[None, :]
-    send_index = (
-        owner_ids * capacity
-        + slot_ids
-        - jnp.sum(jnp.where(owner_match, first_slots[None, :], 0), axis=1)
-    )
-    send_index = jnp.where(is_kept, send_index, slots_all)
-    slot_range = jnp.arange(kept_dev, dtype=jnp.int32)
-    source_ids = kept_pos // tok_dev
-    source_match = source_ids[:, None] == peer_ids[None, :]
-    first_from = jnp.min(jnp.where(source_match, slot_range[:, None], kept_dev), axis=0)
-    recv_index = (
-        source_ids * capacity
-        + slot_range
-        - jnp.sum(jnp.where(source_match, first_from[None, :], 0), axis=1)
-    )
     half_dim = HEAD_DIM // 2
     exponent = jnp.arange(half_dim, dtype=jnp.float32) * (2.0 / HEAD_DIM)
     angles = kept_pos.astype(jnp.float32)[:, None] * (500000.0 ** (-exponent))[None, :]
     cosine, sine = jnp.cos(angles), jnp.sin(angles)
-    later_gain = mlp_gain.astype(jnp.float32)
+    gains = jnp.concatenate(
+        [
+            norm_gain.reshape(8, feature_cols),
+            router_weight.reshape(8, feature_cols),
+            jnp.broadcast_to(mlp_gain, (8, feature_cols)),
+        ]
+    ).astype(jnp.float32)
+    destinations = jnp.broadcast_to(destination, (8, tok_dev))
+    kept_row = jnp.broadcast_to(kept_pos, (8, kept_dev))
+    kept_column = jnp.broadcast_to(kept_pos[:, None], (kept_dev, 128))
     head_share, scaled, score, gate_half, up_half = attend(
         tokens,
-        jnp.broadcast_to(send_index, (8, tok_dev)),
-        jnp.broadcast_to(recv_index[:, None], (kept_dev, 128)),
-        norm_gain.astype(jnp.float32).reshape(8, feature_cols),
-        router_weight.astype(jnp.float32).reshape(8, feature_cols),
+        destinations,
+        kept_row,
+        kept_column,
+        gains,
         query_weight,
         key_weight,
         value_weight,
@@ -1015,22 +1063,22 @@
         up_weight,
         jnp.concatenate([cosine, cosine], axis=1),
         jnp.concatenate([-sine, sine], axis=1),
-        jnp.broadcast_to(later_gain, (8, feature_cols)),
     )
-    return feed_forward(
+    arrived = feed_forward(
         scaled,
         head_share,
         score,
-        jnp.broadcast_to(recv_index, (8, kept_dev)),
-        jnp.broadcast_to(send_index[:, None], (tok_dev, 128)),
-        tokens,
-        jnp.broadcast_to(1.0 / later_gain, (8, feature_cols)),
+        kept_row,
+        kept_column,
+        destinations,
+        gains,
         gate_weight,
         up_weight,
         gate_half,
         up_half,
         down_weight,
     )
+    return (tokens.astype(jnp.float32) + arrived.astype(jnp.float32)).astype(jnp.bfloat16)
 
 
 def solution(mesh):

time: 220 us -> 214 us (0.973)
  local copies, waits for them, and re-layouts: 14.8 us -> 6.02 us
  Pallas kernels: 200 us -> 203 us
    unnamed x19 -> x2, local copies, waits for them, and re-layouts: 10.6 us -> 0.01 us
    convert_element_type x0 -> x2, other arithmetic: none -> 3.24 us  [the longest x1 2.6 us: body(): (tokens.astype(jnp.float32) + arrived.astype(jnp.float32)).astype(jnp.bfl...]
    select_n x3 -> x0, other arithmetic: 2.68 us -> none  [the longest x1 1.33 us: body(): owner_ids = destination // kept_dev]
    broadcast_in_dim x6 -> x4, local copies, waits for them, and re-layouts: 2.79 us -> 4.55 us  [the longest x1 1.33 us: body(): kept_column = jnp.broadcast_to(kept_pos[:, None], (kept_dev, 128))]
where the time goes in v5:
time: 214 us
  Pallas kernels  203 us (95%)
  local copies, waits for them, and re-layouts  6.02 us (3%)
  other arithmetic  4.8 us (2%)
    pallas_call x1, Pallas kernels, feed_forward(): pl.pallas_call(mlp_kernel, out_shape=jax.ShapeDtypeStruct((destination.sh...  117 us
    pallas_call x1, Pallas kernels, attend(): pl.pallas_call(attend_kernel, out_shape=(jax.ShapeDtypeStruct((count, fea...  86.4 us

profile of v5, /device:TPU:32, one launch (start us, length us, event | category | flops | bytes accessed | tf_op | source)
XLA Modules:
  0.0 214.1 jit_solution(18320704792214564348)
XLA Ops:
  0.0 0.7 convert_element_type.17
  0.7 1.3 broadcast_in_dim.18.kept_row_ref
  1.9 1.3 broadcast_in_dim.8.destination_ref
  3.2 0.7 reshape.14
  3.9 0.7 reshape.15
  4.7 0.7 broadcast_in_dim.20
  5.4 1.3 broadcast_in_dim.19.kept_column_ref
  6.7 0.6 maximum_convert_fusion.gains_ref
  7.3 0.2 fusion
  7.5 0.7 pad_maximum_fusion
  8.2 86.4 %attend.1 = (f32[64,1024]{1,0:T(8,128)}, bf16[64,1024]{1,0:T(8,128)(2,1)}, f32[64,128]{1,0:T(8,128)}, bf16[1024,896]{1,0:T(8,128)(2,1)}, bf16[1024,896]{1,0:T(8,128)(2,1)}) custom-call(bf16[512,1024]{1,0:T(8,128)(2,1)} %tokens_ref.1, s32[8,512]{1,0:T(8,128)} %broadcast_in_dim.8.destination_ref, s32[8,64]{1,0:T(8,128)} %broadcast_in_dim.18.kept_row_ref, ...), custom_call_target="tpu_custom_call" | custom-call | tf_op jit(solution)/shard_map/attend/pallas_call | solution.py:970
  94.6 0.0 copy-start
  94.6 116.8 %feed_forward.1 = bf16[512,1024]{1,0:T(8,128)(2,1)} custom-call(bf16[64,1024]{1,0:T(8,128)(2,1)} %get-tuple-element.10.x_ref, f32[64,1024]{1,0:T(8,128)} %get-tuple-element.11.share_ref, f32[64,128]{1,0:T(8,128)} %get-tuple-element.12.score_ref, s32[8,64]{1,0:T(8,128)} %broadcast_in_dim.18.kept_row_ref, s32[64,128]{1,0:T(8,128)} %broadcast_in_dim.19.kept_column_ref, ...), custom_call_target="tpu_custom_call" | custom-call | tf_op jit(solution)/shard_map/feed_forward/pallas_call | solution.py:490
  211.5 0.0 copy-done
  211.5 2.6 %add_convert_fusion = bf16[512,1024]{1,0:T(8,128)(2,1)} fusion(bf16[512,1024]{1,0:T(8,128)(2,1)} %feed_forward.1, bf16[512,1024]{1,0:T(8,128)(2,1)S(1)} %copy-done), kind=kLoop, calls=%fused_computation | loop fusion | flops 2097152 | bytes 3145728 | tf_op jit(solution)/shard_map/convert_element_type | solution.py:1081
  (1 shorter events, 0.0 us)
Async XLA Ops:
  94.6 116.9 %copy-start = (bf16[512,1024]{1,0:T(8,128)(2,1)S(1)}, bf16[512,1024]{1,0:T(8,128)(2,1)}, u32[]{:S(2)}) copy-start(bf16[512,1024]{1,0:T(8,128)(2,1)} %tokens_ref.1) | copy-start | bytes 3145732

commit v6 on v5

--- a/solution.py
+++ b/solution.py
@@ -11,8 +11,8 @@
 VMEM_BYTES = 60 * 2**20
 MESH = pl.DeviceIdType.MESH
 OFFSETS = (
-    (0, 0), (0, 1), (1, 0), (0, 3), (3, 0), (1, 1), (3, 3), (1, 3),
-    (3, 1), (0, 2), (2, 0), (1, 2), (2, 1), (3, 2), (2, 3), (2, 2),
+    (0, 0), (0, 1), (1, 0), (0, 3), (3, 0), (0, 2), (2, 0), (1, 1),
+    (3, 3), (1, 3), (3, 1), (1, 2), (2, 1), (3, 2), (2, 3), (2, 2),
 )
 EPS = 1e-05
 
@@ -90,6 +90,8 @@
     swap_recv,
     x_send,
     x_recv,
+    half_send,
+    half_recv,
     pass_send,
     pass_recv,
     far_send,
@@ -174,13 +176,41 @@
             own_x.at[place], sib_x.at[place], pass_send.at[who], pass_recv.at[who], sibling
         )
 
-    for k in range(1, 4):
+    short = rows // 2
+
+    def half_copy(dx, dy, side):
+        slot = OFFSETS.index((dx, dy))
+        source = OFFSETS.index((0, dy) if side else (dx, 0))
+        to = lax.rem(x + 4 - dx, 4) * 4 + y if side else x * 4 + lax.rem(y + 4 - dy, 4)
+        return remote(
+            own_x.at[pl.ds(source * rows + side * short, short)],
+            own_x.at[pl.ds(slot * rows + side * short, short)],
+            half_send.at[side * 16 + slot],
+            half_recv.at[side * 16 + slot],
+            (to, m),
+        )
+
+    def half_in(slot, side):
+        start = pl.multiple_of(slot * rows + side * short, short)
+        return remote(
+            own_x.at[pl.ds(0, short)],
+            own_x.at[pl.ds(start, short)],
+            half_send.at[0],
+            half_recv.at[side * 16 + slot],
+            sibling,
+        )
+
+    def halves(slot):
+        dx, dy = OFFSETS[slot]
+        if dx:
+            return [half_copy(dx, k, 0) for k in range(1, 4)]
+        return [half_copy(k, dy, 1) for k in range(1, 4)]
+
+    for k in range(1, 7):
         x_copy(k).start()
     gain_swap = remote(own_gain, sib_gain, swap_send.at[0], swap_recv.at[0], sibling)
     x_pass(0).start()
     gain_swap.start()
-
-    short = rows // 2
 
     def near(way):
         return z_peer(1 + 2 * way)
@@ -273,17 +303,26 @@
         def _(k):
             slot = turn * 4 + k
 
+            @pl.when((slot > 0) & (slot < 7))
+            def _():
+                x_in(slot).wait_recv()
+
+            @pl.when(slot >= 7)
+            def _():
+                half_in(slot, 0).wait_recv()
+                half_in(slot, 1).wait_recv()
+
             @pl.when(slot > 0)
             def _():
-                x_in(slot).wait_recv()
                 x_pass(slot).start()
 
-        for t in range(3):
+        for t in range(2):
 
             @pl.when(turn == t)
             def _():
-                for k in range(4 * t + 4, 4 * t + 8):
-                    x_copy(k).start()
+                for slot in range(3 * t + 1, 3 * t + 4):
+                    for copy in halves(slot):
+                        copy.start()
 
         @pl.when(turn == 0)
         def _():
@@ -446,8 +485,11 @@
             back_to, inbox[:, cols], preferred_element_type=jnp.float32
         ).astype(jnp.bfloat16)
 
+    for k in range(1, 7):
+        x_copy(k).wait_send()
+        for copy in halves(k):
+            copy.wait_send()
     for k in range(1, 16):
-        x_copy(k).wait_send()
         out_in(k).wait_send()
         box_copy(k).wait_send()
 
@@ -512,8 +554,12 @@
             dma((5,)),
             dma((1,)),
             dma((1,)),
+            dma((16,)),
+            dma((16,)),
+            dma((32,)),
+            dma((32,)),
         ]
-        + [dma((16,))] * 20,
+        + [dma((16,))] * 18,
         compiler_params=pltpu.CompilerParams(
             collective_id=3, has_side_effects=True, vmem_limit_bytes=VMEM_BYTES
         ),

time: 214 us -> 211 us (0.986); the launches traced: 214 us -> 208 us
  Pallas kernels: 203 us -> 197 us
    pallas_call x1, Pallas kernels: 117 us -> 111 us  [feed_forward(): pl.pallas_call(mlp_kernel, out_shape=jax.ShapeDtypeStruct((destination.sh...]
where the time goes in v6:
time: 211 us; the launch traced here: 208 us
  Pallas kernels  197 us (93%)
  local copies, waits for them, and re-layouts  6.02 us (3%)
  other arithmetic  4.8 us (2%)
    pallas_call x1, Pallas kernels, feed_forward(): pl.pallas_call(mlp_kernel, out_shape=jax.ShapeDtypeStruct((destination.sh...  111 us
    pallas_call x1, Pallas kernels, attend(): pl.pallas_call(attend_kernel, out_shape=(jax.ShapeDtypeStruct((count, fea...  86.3 us

profile of v6, /device:TPU:32, one launch (start us, length us, event | category | flops | bytes accessed | tf_op | source)
XLA Modules:
  0.0 207.9 jit_solution(5595105063322682899)
XLA Ops:
  0.0 0.7 convert_element_type.17
  0.7 1.3 broadcast_in_dim.18.kept_row_ref
  1.9 1.3 broadcast_in_dim.8.destination_ref
  3.2 0.7 reshape.14
  3.9 0.7 reshape.15
  4.7 0.7 broadcast_in_dim.20
  5.4 1.3 broadcast_in_dim.19.kept_column_ref
  6.7 0.6 maximum_convert_fusion.gains_ref
  7.3 0.2 fusion
  7.5 0.7 pad_maximum_fusion
  8.2 86.3 %attend.1 = (f32[64,1024]{1,0:T(8,128)}, bf16[64,1024]{1,0:T(8,128)(2,1)}, f32[64,128]{1,0:T(8,128)}, bf16[1024,896]{1,0:T(8,128)(2,1)}, bf16[1024,896]{1,0:T(8,128)(2,1)}) custom-call(bf16[512,1024]{1,0:T(8,128)(2,1)} %tokens_ref.1, s32[8,512]{1,0:T(8,128)} %broadcast_in_dim.8.destination_ref, s32[8,64]{1,0:T(8,128)} %broadcast_in_dim.18.kept_row_ref, ...), custom_call_target="tpu_custom_call" | custom-call | tf_op jit(solution)/shard_map/attend/pallas_call | solution.py:1016
  94.6 0.0 copy-start
  94.6 110.7 %feed_forward.1 = bf16[512,1024]{1,0:T(8,128)(2,1)} custom-call(bf16[64,1024]{1,0:T(8,128)(2,1)} %get-tuple-element.10.x_ref, f32[64,1024]{1,0:T(8,128)} %get-tuple-element.11.share_ref, f32[64,128]{1,0:T(8,128)} %get-tuple-element.12.score_ref, s32[8,64]{1,0:T(8,128)} %broadcast_in_dim.18.kept_row_ref, s32[64,128]{1,0:T(8,128)} %broadcast_in_dim.19.kept_column_ref, ...), custom_call_target="tpu_custom_call" | custom-call | tf_op jit(solution)/shard_map/feed_forward/pallas_call | solution.py:532
  205.3 0.0 copy-done
  205.3 2.6 %add_convert_fusion = bf16[512,1024]{1,0:T(8,128)(2,1)} fusion(bf16[512,1024]{1,0:T(8,128)(2,1)} %feed_forward.1, bf16[512,1024]{1,0:T(8,128)(2,1)S(1)} %copy-done), kind=kLoop, calls=%fused_computation | loop fusion | flops 2097152 | bytes 3145728 | tf_op jit(solution)/shard_map/convert_element_type | solution.py:1127
  (1 shorter events, 0.0 us)
Async XLA Ops:
  94.6 110.7 %copy-start = (bf16[512,1024]{1,0:T(8,128)(2,1)S(1)}, bf16[512,1024]{1,0:T(8,128)(2,1)}, u32[]{:S(2)}) copy-start(bf16[512,1024]{1,0:T(8,128)(2,1)} %tokens_ref.1) | copy-start | bytes 3145732

commit v7 on v6

--- a/solution.py
+++ b/solution.py
@@ -782,9 +782,6 @@
     for k in (0, 1, 3, 2):
         hop(z_sibling(k)).wait_recv()
 
-    for k in (1, 3):
-        weight_copy(k).wait_recv()
-        weight_lap(k).start()
     square, route = 0.0, 0.0
     for at in range(8):
         wide = full[at].astype(jnp.float32)
@@ -811,6 +808,9 @@
         norm_copy(k).start()
     blocks[0, 0] = normed[2 * x]
     blocks[1, 0] = normed[2 * x + 1]
+    for k in (1, 3):
+        weight_copy(k).wait_recv()
+        weight_lap(k).start()
     half = gate_half_ref.shape[1]
     others = pl.ds(pl.multiple_of((1 - core) * half, 128), half)
     swaps = [
@@ -889,8 +889,8 @@
         (((1,), (1,)), ((), ())),
         preferred_element_type=jnp.float32,
     ) * (HEAD_DIM ** (-0.5))
-    query_at = lax.broadcasted_iota(jnp.int32, (heads * rows, keys), 0) % rows * 16 + c
-    key_at = lax.broadcasted_iota(jnp.int32, (heads * rows, keys), 1)
+    query_at = lax.broadcasted_iota(jnp.int32, (heads * rows, 1), 0) % rows * 16 + c
+    key_at = lax.broadcasted_iota(jnp.int32, (1, keys), 1)
     allowed = key_at % rows * 16 + key_at // rows <= query_at
     scores = jnp.where(allowed, scores, -1e30)
     weights = jnp.exp(scores - jnp.max(scores, axis=1, keepdims=True))

time: 211 us -> 206 us (0.976)
  Pallas kernels: 197 us -> 193 us
    pallas_call x1, Pallas kernels: 86.3 us -> 83.2 us  [attend(): pl.pallas_call(attend_kernel, out_shape=(jax.ShapeDtypeStruct((count, fea...]
where the time goes in v7:
time: 206 us; the launch traced here: 204 us
  Pallas kernels  193 us (94%)
  local copies, waits for them, and re-layouts  6.02 us (3%)
  other arithmetic  4.8 us (2%)
    pallas_call x1, Pallas kernels, feed_forward(): pl.pallas_call(mlp_kernel, out_shape=jax.ShapeDtypeStruct((destination.sh...  110 us
    pallas_call x1, Pallas kernels, attend(): pl.pallas_call(attend_kernel, out_shape=(jax.ShapeDtypeStruct((count, fea...  83.2 us

profile of v7, /device:TPU:32, one launch (start us, length us, event | category | flops | bytes accessed | tf_op | source)
XLA Modules:
  0.0 204.3 jit_solution(16428379712284763564)
XLA Ops:
  0.0 0.7 convert_element_type.17
  0.7 1.3 broadcast_in_dim.18.kept_row_ref
  1.9 1.3 broadcast_in_dim.8.destination_ref
  3.2 0.7 reshape.14
  3.9 0.7 reshape.15
  4.7 0.7 broadcast_in_dim.20
  5.4 1.3 broadcast_in_dim.19.kept_column_ref
  6.7 0.6 maximum_convert_fusion.gains_ref
  7.3 0.2 fusion
  7.5 0.7 pad_maximum_fusion
  8.2 83.2 %attend.1 = (f32[64,1024]{1,0:T(8,128)}, bf16[64,1024]{1,0:T(8,128)(2,1)}, f32[64,128]{1,0:T(8,128)}, bf16[1024,896]{1,0:T(8,128)(2,1)}, bf16[1024,896]{1,0:T(8,128)(2,1)}) custom-call(bf16[512,1024]{1,0:T(8,128)(2,1)} %tokens_ref.1, s32[8,512]{1,0:T(8,128)} %broadcast_in_dim.8.destination_ref, s32[8,64]{1,0:T(8,128)} %broadcast_in_dim.18.kept_row_ref, ...), custom_call_target="tpu_custom_call" | custom-call | tf_op jit(solution)/shard_map/attend/pallas_call | solution.py:1016
  91.5 0.0 copy-start
  91.5 110.2 %feed_forward.1 = bf16[512,1024]{1,0:T(8,128)(2,1)} custom-call(bf16[64,1024]{1,0:T(8,128)(2,1)} %get-tuple-element.10.x_ref, f32[64,1024]{1,0:T(8,128)} %get-tuple-element.11.share_ref, f32[64,128]{1,0:T(8,128)} %get-tuple-element.12.score_ref, s32[8,64]{1,0:T(8,128)} %broadcast_in_dim.18.kept_row_ref, s32[64,128]{1,0:T(8,128)} %broadcast_in_dim.19.kept_column_ref, ...), custom_call_target="tpu_custom_call" | custom-call | tf_op jit(solution)/shard_map/feed_forward/pallas_call | solution.py:532
  201.7 0.0 copy-done
  201.7 2.6 %add_convert_fusion = bf16[512,1024]{1,0:T(8,128)(2,1)} fusion(bf16[512,1024]{1,0:T(8,128)(2,1)} %feed_forward.1, bf16[512,1024]{1,0:T(8,128)(2,1)S(1)} %copy-done), kind=kLoop, calls=%fused_computation | loop fusion | flops 2097152 | bytes 3145728 | tf_op jit(solution)/shard_map/convert_element_type | solution.py:1127
  (1 shorter events, 0.0 us)
Async XLA Ops:
  91.5 110.2 %copy-start = (bf16[512,1024]{1,0:T(8,128)(2,1)S(1)}, bf16[512,1024]{1,0:T(8,128)(2,1)}, u32[]{:S(2)}) copy-start(bf16[512,1024]{1,0:T(8,128)(2,1)} %tokens_ref.1) | copy-start | bytes 3145732

commit v8 on v7

--- a/solution.py
+++ b/solution.py
@@ -811,6 +811,8 @@
     for k in (1, 3):
         weight_copy(k).wait_recv()
         weight_lap(k).start()
+    for k in (1, 3):
+        out_weight_copy(k).start()
     half = gate_half_ref.shape[1]
     others = pl.ds(pl.multiple_of((1 - core) * half, 128), half)
     swaps = [
@@ -827,8 +829,6 @@
         norm_copy(k).wait_recv()
     for k in (1, 3):
         weight_lap(k).wait_recv()
-    for k in (1, 3):
-        out_weight_copy(k).start()
 
     @pl.loop(0, cols // 256)
     def _(tile):

time: 206 us -> 206 us (level)
    pallas_call x1, Pallas kernels: 110 us -> 112 us  [feed_forward(): pl.pallas_call(mlp_kernel, out_shape=jax.ShapeDtypeStruct((destination.sh...]
where the time goes in v8:
time: 206 us; the launch traced here: 205 us
  Pallas kernels  194 us (94%)
  local copies, waits for them, and re-layouts  6.02 us (3%)
  other arithmetic  4.8 us (2%)
    pallas_call x1, Pallas kernels, feed_forward(): pl.pallas_call(mlp_kernel, out_shape=jax.ShapeDtypeStruct((destination.sh...  112 us
    pallas_call x1, Pallas kernels, attend(): pl.pallas_call(attend_kernel, out_shape=(jax.ShapeDtypeStruct((count, fea...  81.2 us

profile of v8, /device:TPU:32, one launch (start us, length us, event | category | flops | bytes accessed | tf_op | source)
XLA Modules:
  0.0 204.5 jit_solution(1346753960816055953)
XLA Ops:
  0.0 0.7 convert_element_type.17
  0.7 1.3 broadcast_in_dim.18.kept_row_ref
  1.9 1.3 broadcast_in_dim.8.destination_ref
  3.2 0.7 reshape.14
  3.9 0.7 reshape.15
  4.7 0.7 broadcast_in_dim.20
  5.4 1.3 broadcast_in_dim.19.kept_column_ref
  6.7 0.6 maximum_convert_fusion.gains_ref
  7.3 0.2 fusion
  7.5 0.7 pad_maximum_fusion
  8.2 81.2 %attend.1 = (f32[64,1024]{1,0:T(8,128)}, bf16[64,1024]{1,0:T(8,128)(2,1)}, f32[64,128]{1,0:T(8,128)}, bf16[1024,896]{1,0:T(8,128)(2,1)}, bf16[1024,896]{1,0:T(8,128)(2,1)}) custom-call(bf16[512,1024]{1,0:T(8,128)(2,1)} %tokens_ref.1, s32[8,512]{1,0:T(8,128)} %broadcast_in_dim.8.destination_ref, s32[8,64]{1,0:T(8,128)} %broadcast_in_dim.18.kept_row_ref, ...), custom_call_target="tpu_custom_call" | custom-call | tf_op jit(solution)/shard_map/attend/pallas_call | solution.py:1016
  89.4 0.0 copy-start
  89.5 112.5 %feed_forward.1 = bf16[512,1024]{1,0:T(8,128)(2,1)} custom-call(bf16[64,1024]{1,0:T(8,128)(2,1)} %get-tuple-element.10.x_ref, f32[64,1024]{1,0:T(8,128)} %get-tuple-element.11.share_ref, f32[64,128]{1,0:T(8,128)} %get-tuple-element.12.score_ref, s32[8,64]{1,0:T(8,128)} %broadcast_in_dim.18.kept_row_ref, s32[64,128]{1,0:T(8,128)} %broadcast_in_dim.19.kept_column_ref, ...), custom_call_target="tpu_custom_call" | custom-call | tf_op jit(solution)/shard_map/feed_forward/pallas_call | solution.py:532
  201.9 0.0 copy-done
  201.9 2.6 %add_convert_fusion = bf16[512,1024]{1,0:T(8,128)(2,1)} fusion(bf16[512,1024]{1,0:T(8,128)(2,1)} %feed_forward.1, bf16[512,1024]{1,0:T(8,128)(2,1)S(1)} %copy-done), kind=kLoop, calls=%fused_computation | loop fusion | flops 2097152 | bytes 3145728 | tf_op jit(solution)/shard_map/convert_element_type | solution.py:1127
  (1 shorter events, 0.0 us)
Async XLA Ops:
  89.4 112.5 %copy-start = (bf16[512,1024]{1,0:T(8,128)(2,1)S(1)}, bf16[512,1024]{1,0:T(8,128)(2,1)}, u32[]{:S(2)}) copy-start(bf16[512,1024]{1,0:T(8,128)(2,1)} %tokens_ref.1) | copy-start | bytes 3145732
